TPU v7x, 512 devices: a whole 4x8x8 slice. The times are simulated.
512 devices in a mesh: seq: 32 (over x, y_hi, core), dp: 16 (over z, y_lo).
Axes of the slice: x: 4, y: 8 (y_hi: 4, y_lo: 2; y = y_hi * 2 + y_lo), z: 8, core: 2. Of those that a mesh axis runs over, the one named last changes fastest.
Arguments:
- queries: bfloat16 [16, 4096, 2048], P('dp', 'seq'), may hold values from -6 to 6
- key_branch: bfloat16 [16, 4096, 2048], P('dp', 'seq'), may hold values from -6 to 6
- value_branch: bfloat16 [16, 4096, 2048], P('dp', 'seq'), may hold values from -6 to 6
- cotangent: bfloat16 [16, 4096, 2048], P('dp', 'seq'), may hold values from -6 to 6
- residues: float32 [16, 2048], replicated, may hold values from -0.046875 to 0.046875
- rates: float32 [16, 2048], replicated, may hold values from 0.2 to 300
- skip_gain: float32 [2048], replicated, may hold values from 0.5 to 1.5
Outputs:
- grad_query: bfloat16 [16, 4096, 2048], P('dp', 'seq')
- grad_key: bfloat16 [16, 4096, 2048], P('dp', 'seq')
- grad_value: bfloat16 [16, 4096, 2048], P('dp', 'seq')
- grad_residue: float32 [16, 2048], P(None, 'seq')
- grad_lograte: float32 [16, 2048], P(None, 'seq')
- grad_skip: float32 [2048], P('seq')
All inputs are finite; a program needn't handle non-finite values.
Results may differ from a plain program's by a relative error of at most 0.01.
Values may be sent and summed in bfloat16 or wider, within the bound.
A program may use at most 128 MiB of HBM per device.

v0:
```python
import math

import jax
import jax.numpy as jnp
from jax import lax
from jax.sharding import PartitionSpec as P

highish = lax.Precision.HIGH


def dft_table(period, rows, cols):
    left = jnp.arange(rows, dtype=jnp.int32)[:, None]
    right = jnp.arange(cols, dtype=jnp.int32)[None, :]
    angle = 2.0 * math.pi / period * (left * right % period).astype(jnp.float32)
    return (jnp.cos(angle), jnp.sin(angle))


def forward(real_in, imag_in):
    width, length = real_in.shape
    total = 2 * length
    blocks = total // 128
    half = blocks // 2
    cos_a, sin_a = dft_table(blocks, blocks, half)
    if imag_in is None:
        table = jnp.concatenate([cos_a, -sin_a], axis=0)
        stacked = real_in.reshape(width, half, 128)
    else:
        upper = jnp.concatenate([cos_a, sin_a], axis=1)
        lower = jnp.concatenate([-sin_a, cos_a], axis=1)
        table = jnp.concatenate([upper, lower], axis=0)
        stacked = jnp.concatenate(
            [real_in.reshape(width, half, 128), imag_in.reshape(width, half, 128)], axis=1
        )
    section = jnp.einsum("ra,wab->wrb", table, stacked, precision=highish)
    real_y = section[:, :blocks]
    imag_y = section[:, blocks:]
    cos_t, sin_t = dft_table(total, blocks, 128)
    real_w = real_y * cos_t + imag_y * sin_t
    imag_w = imag_y * cos_t - real_y * sin_t
    joined = jnp.concatenate([real_w, imag_w], axis=2)
    cos_b, sin_b = dft_table(128, 128, 128)
    second = jnp.concatenate(
        [jnp.concatenate([cos_b, -sin_b], axis=1), jnp.concatenate([sin_b, cos_b], axis=1)], axis=0
    )
    return jnp.einsum("wcb,be->wce", joined, second, precision=highish)


def inverse(spec, both):
    width, blocks, lanes = spec.shape
    total = blocks * 128
    half = blocks // 2
    cos_b, sin_b = dft_table(128, 128, 128)
    third = jnp.concatenate(
        [jnp.concatenate([cos_b, sin_b], axis=1), jnp.concatenate([-sin_b, cos_b], axis=1)], axis=0
    )
    section = jnp.einsum("wcd,de->wce", spec, third, precision=highish)
    real_g = section[..., :128]
    imag_g = section[..., 128:]
    cos_t, sin_t = dft_table(total, blocks, 128)
    real_h = real_g * cos_t - imag_g * sin_t
    imag_h = imag_g * cos_t + real_g * sin_t
    stacked = jnp.concatenate([real_h, imag_h], axis=1)
    cos_a, sin_a = dft_table(blocks, blocks, half)
    real_rows = jnp.concatenate([cos_a.T, -sin_a.T], axis=1)
    if both:
        imag_rows = jnp.concatenate([sin_a.T, cos_a.T], axis=1)
        table = jnp.concatenate([real_rows, imag_rows], axis=0)
    else:
        table = real_rows
    out = jnp.einsum("ac,wcb->wab", table, stacked, precision=highish) / jnp.float32(total)
    if both:
        return (out[:, :half].reshape(width, total // 2), out[:, half:].reshape(width, total // 2))
    return out.reshape(width, total // 2)


def mirrored(values):
    flip_c = jnp.roll(jnp.flip(values, 1), 1, axis=1)
    flip_d = jnp.flip(flip_c, 2)
    return jnp.concatenate([jnp.roll(flip_d[:, :1], 1, axis=2), flip_d[:, 1:]], axis=1)


def unpack(spec):
    real_z = spec[..., :128]
    imag_z = spec[..., 128:]
    real_r = mirrored(real_z)
    imag_r = -mirrored(imag_z)
    first = (0.5 * (real_z + real_r), 0.5 * (imag_z + imag_r))
    second = (0.5 * (imag_z - imag_r), -0.5 * (real_z - real_r))
    return (first, second)


def split_spec(spec):
    return (spec[..., :128], spec[..., 128:])


def times_spec(first, second, conj_first):
    real_a, imag_a = first
    real_b, imag_b = second
    if conj_first:
        imag_a = -imag_a
    return (real_a * real_b - imag_a * imag_b, real_a * imag_b + imag_a * real_b)


def shards(queries, key_branch, value_branch, cotangent, residues, rates, skip_gain):
    groups = lax.axis_size("seq")
    rank_seq = lax.axis_index("seq")
    tok_rows = queries.shape[1]
    channels = queries.shape[2]
    width = channels // groups
    length = tok_rows * groups
    scale = jnp.float32(length)
    key_f = key_branch.astype(jnp.float32)
    value_f = value_branch.astype(jnp.float32)
    product = (key_f * value_f).astype(jnp.bfloat16)
    carried = (cotangent.astype(jnp.float32) * queries.astype(jnp.float32)).astype(jnp.bfloat16)
    first_chan = rank_seq * width
    res_own = lax.dynamic_slice_in_dim(residues, first_chan, width, 1)
    decay_own = lax.dynamic_slice_in_dim(rates, first_chan, width, 1) / scale
    steps_f = jnp.arange(length, dtype=jnp.float32)
    taps = jnp.sum(
        res_own[:, :, None] * jnp.exp(-decay_own[:, :, None] * steps_f[None, None, :]), axis=0
    )
    prod_send = product[0].T
    carr_send = carried[0].T
    prod_cols, carr_cols = (
        lax.all_to_all(prod_send, "seq", split_axis=0, concat_axis=1, tiled=True),
        lax.all_to_all(carr_send, "seq", split_axis=0, concat_axis=1, tiled=True),
    )
    joint = forward(prod_cols.astype(jnp.float32), carr_cols.astype(jnp.float32))
    prod_spec, carr_spec = unpack(joint)
    filt_spec = split_spec(forward(taps, None))
    real_u, imag_u = times_spec(prod_spec, filt_spec, False)
    real_v, imag_v = times_spec(filt_spec, carr_spec, True)
    both_spec = jnp.concatenate([real_u - imag_v, imag_u + real_v], axis=2)
    conv_cols, back_cols = inverse(both_spec, True)
    lag_real, lag_imag = times_spec(prod_spec, carr_spec, True)
    lagged = inverse(jnp.concatenate([lag_real, lag_imag], axis=2), False)
    conv_home, back_home = (
        lax.all_to_all(
            conv_cols.astype(jnp.bfloat16), "seq", split_axis=1, concat_axis=0, tiled=True
        ),
        lax.all_to_all(
            back_cols.astype(jnp.bfloat16), "seq", split_axis=1, concat_axis=0, tiled=True
        ),
    )
    weighted = jnp.stack([lagged, lagged * steps_f[None, :]])
    sums = jnp.sum(
        jnp.exp(-decay_own[None, :, :, None] * steps_f[None, None, None, :]) * weighted[:, None],
        axis=3,
    )
    res_part = sums[0]
    log_part = -res_own * decay_own * sums[1]
    skip_terms = jnp.sum(carried.astype(jnp.float32) * product.astype(jnp.float32), axis=(0, 1))
    skip_local = lax.psum_scatter(skip_terms, "seq", scatter_dimension=0, tiled=True)
    conv_full = conv_home.T[None].astype(jnp.float32)
    back_full = back_home.T[None].astype(jnp.float32)
    grad_res, grad_log, grad_skp = lax.psum((res_part, log_part, skip_local), "dp")
    gain = skip_gain[None, None, :]
    grad_query = (
        cotangent.astype(jnp.float32) * (conv_full + gain * product.astype(jnp.float32))
    ).astype(jnp.bfloat16)
    dz_full = back_full + gain * carried.astype(jnp.float32)
    grad_key = (dz_full * value_f).astype(jnp.bfloat16)
    grad_value = (dz_full * key_f).astype(jnp.bfloat16)
    return (grad_query, grad_key, grad_value, grad_res / scale, grad_log / scale, grad_skp / scale)


def solution(mesh):
    in_specs = (
        P("dp", "seq", None),
        P("dp", "seq", None),
        P("dp", "seq", None),
        P("dp", "seq", None),
        P(),
        P(),
        P(),
    )
    out_specs = (
        P("dp", "seq", None),
        P("dp", "seq", None),
        P("dp", "seq", None),
        P(None, "seq"),
        P(None, "seq"),
        P("seq"),
    )
    return jax.shard_map(shards, mesh=mesh, in_specs=in_specs, out_specs=out_specs, check_vma=False)
```

profile of v0, /device:TPU:6, one launch (start us, length us, event | category | flops | bytes accessed | tf_op | source)
XLA Modules:
  0.0 279.1 jit_solution(5457941999861756413)
XLA Ops:
  0.7 1.4 copy.35
  2.1 1.5 copy.36
  4.2 1.3 fusion.42
  5.5 10.2 %all-to-all-start.1 = ((bf16[32,64,128]{2,1,0:T(8,128)(2,1)}), bf16[32,64,128]{2,1,0:T(8,128)(2,1)S(1)}, u32[]{:S(2)}, u32[]{:S(2)}) async-start(bf16[32,64,128]{2,1,0:T(8,128)(2,1)} %bitcast.6), calls=%async_computation.1 | async-start | bytes 1048576 | tf_op jit(solution)/shard_map/all_to_all | solution.py:127
  15.8 0.8 fusion.106
  16.6 6.9 %multiply_exponential_fusion = (f32[16,64,4096]{2,1,0:T(8,128)}, f32[64,4096]{1,0:T(8,128)S(1)}) fusion(f32[16,64]{1,0:T(8,128)S(1)} %get-tuple-element.63, f32[16,64]{1,0:T(8,128)S(1)} %get-tuple-element.64), kind=kLoop, calls=%fused_computation.2 | loop fusion | flops 12320768 | bytes 17833984 | tf_op jit(solution)/shard_map/exp | solution.py:121
  23.7 1.3 dynamic-slice
  25.6 64.8 %all-reduce = f32[2048]{0:T(1024)S(1)} all-reduce(f32[2048]{0:T(1024)S(1)} %get-tuple-element.27), channel_id=2, replica_groups=mesh['seq'=32,'dp'=16] {'seq'}, use_global_device_ids=true, to_apply=%region_5.6.clone | all-reduce | flops 2048 | bytes 16384
  90.6 15.8 %all-to-all-start = ((bf16[32,64,128]{2,1,0:T(8,128)(2,1)}), bf16[32,64,128]{2,1,0:T(8,128)(2,1)S(1)}, u32[]{:S(2)}, u32[]{:S(2)}) async-start(bf16[32,64,128]{2,1,0:T(8,128)(2,1)} %bitcast.2), calls=%async_computation | async-start | bytes 1048576 | tf_op jit(solution)/shard_map/all_to_all | solution.py:126
  107.4 3.8 %convolution_bitcast_fusion = f32[64,128,128]{2,1,0:T(8,128)} fusion(f32[64,32,128]{2,1,0:T(8,128)S(1)} %bitcast.74, f32[64,32]{0,1:T(8,128)S(1)} %get-tuple-element.66, f32[64,32]{0,1:T(8,128)S(1)} %get-tuple-element.65), kind=kOutput, calls=%fused_computation.27 | convolution fusion | flops 201330688 | bytes 5259264 | tf_op jit(solution)/shard_map/ra,wab->wrb/dot_general | solution.py:34
  111.2 0.3 copy.49
  111.6 11.5 %all-to-all-done = bf16[32,64,128]{2,1,0:T(8,128)(2,1)S(1)} async-done(((bf16[32,64,128]{2,1,0:T(8,128)(2,1)}), bf16[32,64,128]{2,1,0:T(8,128)(2,1)S(1)}, u32[]{:S(2)}, u32[]{:S(2)}) %all-to-all-start) | async-done | bytes 524320 | tf_op jit(solution)/shard_map/all_to_all | solution.py:126
  123.1 0.3 copy.50
  123.4 1.4 convolution_bitcast_fusion.1
  124.8 0.8 copy-done.2
  125.6 3.5 %multiply_add_fusion.3 = (f32[64,64,128]{2,1,0:T(8,128)}, f32[64,64,128]{2,1,0:T(8,128)}, f32[64,64,128]{2,1,0:T(8,128)S(1)}, f32[64,64,128]{2,1,0:T(8,128)S(1)}) fusion(f32[64,128,128]{2,1,0:T(8,128)S(1)} %copy-done.2, f32[64,128]{1,0:T(8,128)S(1)} %get-tuple-element.67, f32[64,128]{1,0:T(8,128)S(1)} %get-tuple-element.68, ...), kind=kLoop, calls=%fused_computation.45 | loop fusion | flops 6291456 | bytes 16842752 | tf_op jit(solution)/shard_map/add | solution.py:38
  129.1 1.8 fusion
  131.0 3.1 %fusion.120 = (f32[64,63,128]{2,1,0:T(8,128)}, f32[64,63,128]{2,1,0:T(8,128)}) fusion(f32[64,64,256]{2,1,0:T(8,128)S(1)} %fusion), kind=kLoop, calls=%fused_computation.169 | loop fusion | bytes 8257536 | tf_op jit(solution)/shard_map/jit(_roll_static)/slice | solution.py:77
  134.3 3.5 %slice.113 = f32[64,63,128]{2,1,0:T(8,128)S(1)} reverse(f32[64,63,128]{2,1,0:T(8,128)} %get-tuple-element.51), dimensions={1,2} | reverse | bytes 4128768 | tf_op jit(solution)/shard_map/slice | solution.py:79
  137.8 4.5 %slice.122 = f32[64,63,128]{2,1,0:T(8,128)} reverse(f32[64,63,128]{2,1,0:T(8,128)} %get-tuple-element.50), dimensions={1,2} | reverse | bytes 4128768 | tf_op jit(solution)/shard_map/slice | solution.py:79
  142.3 0.3 slice.111
  142.6 0.3 slice.120
  142.9 4.3 %fusion.4 = f32[64,64,256]{2,1,0:T(8,128)S(1)} fusion(f32[64,64,128]{2,1,0:T(8,128)} %get-tuple-element.43, f32[64,64,128]{2,1,0:T(8,128)} %get-tuple-element.42, f32[128,128]{1,0:T(8,128)S(1)} %get-tuple-element.70, f32[128,128]{1,0:T(8,128)S(1)} %get-tuple-element.69, f32[128,128]{1,0:T(8,128)S(1)} %fusion.80), kind=kOutput, calls=%fused_computation.7 | convolution fusion | flops 1611857920 | bytes 8585216 | tf_op jit(solution)/shard_map/wcb,be->wce/dot_general | solution.py:45
  147.2 1.5 multiply_subtract_fusion.1
  148.6 2.1 add_subtract_fusion
  150.7 1.9 fusion.8
  152.6 1.9 fusion.16
  154.5 2.3 multiply_subtract_fusion
  156.8 2.2 fusion.32
  159.0 1.4 stack_reshape.3
  160.4 1.1 iota_multiply_fusion
  161.5 0.9 copy-done.4
  162.4 1.4 fusion.26
  163.9 1.0 copy.41
  164.9 6.5 %all-to-all-start.2 = ((bf16[64,32,128]{2,0,1:T(8,128)(2,1)}), bf16[64,32,128]{2,0,1:T(8,128)(2,1)S(1)}, u32[]{:S(2)}, u32[]{:S(2)}) async-start(bf16[64,32,128]{2,0,1:T(8,128)(2,1)} %copy.41), calls=%async_computation.2 | async-start | bytes 1048576 | tf_op jit(solution)/shard_map/all_to_all | solution.py:139
  171.5 1.0 copy.42
  172.5 9.8 %multiply_reduce_fusion = f32[2,16,64]{2,1,0:T(8,128)S(1)} fusion(f32[2,64,4096]{2,1,0:T(8,128)S(1)} %pad_maximum_fusion.1, f32[16,64,4096]{2,1,0:T(8,128)} %get-tuple-element.60), kind=kLoop, calls=%fused_computation | loop fusion | flops 16775168 | bytes 18882560 | tf_op jit(solution)/shard_map/reduce_sum | solution.py:147
  182.4 5.1 %all-to-all-done.2 = bf16[64,32,128]{2,0,1:T(8,128)(2,1)S(1)} async-done(((bf16[64,32,128]{2,0,1:T(8,128)(2,1)}), bf16[64,32,128]{2,0,1:T(8,128)(2,1)S(1)}, u32[]{:S(2)}, u32[]{:S(2)}) %all-to-all-start.2) | async-done | bytes 524320 | tf_op jit(solution)/shard_map/all_to_all | solution.py:139
  187.5 6.8 %all-to-all-start.3 = ((bf16[64,32,128]{2,0,1:T(8,128)(2,1)}), bf16[64,32,128]{2,0,1:T(8,128)(2,1)S(1)}, u32[]{:S(2)}, u32[]{:S(2)}) async-start(bf16[64,32,128]{2,0,1:T(8,128)(2,1)} %copy.42), calls=%async_computation.3 | async-start | bytes 1048576 | tf_op jit(solution)/shard_map/all_to_all | solution.py:142
  194.3 0.8 fusion.99
  195.1 74.3 %all-reduce.1 = (f32[16,64]{1,0:T(8,128)S(1)}, f32[16,64]{1,0:T(8,128)S(1)}, f32[64]{0:T(128)S(1)}) all-reduce(f32[16,64]{1,0:T(8,128)S(1)} %slice_bitcast_fusion.1, f32[16,64]{1,0:T(8,128)S(1)} %fusion.99, f32[64]{0:T(128)S(1)} %dynamic-slice.1), channel_id=1, replica_groups=mesh['seq'=32,'dp'=16] {'dp'}, use_global_device_ids=true, to_apply=%region_2.3 | all-reduce | flops 2112 | bytes 16896 | tf_op jit(solution)/shard_map/psum | solution.py:157
  269.4 0.5 broadcast_multiply_fusion.2
  269.9 0.6 broadcast_multiply_fusion
  270.5 0.6 broadcast_multiply_fusion.1
  271.2 2.8 %fusion.37 = (bf16[1,128,2048]{1,2,0:T(8,128)(2,1)S(1)}, bf16[1,128,2048]{1,2,0:T(8,128)(2,1)}, bf16[1,128,2048]{1,2,0:T(8,128)(2,1)}) fusion(bf16[1,128,2048]{1,2,0:T(8,128)(2,1)S(1)} %copy-done.8, bf16[1,128,2048]{1,2,0:T(8,128)(2,1)} %get-tuple-element.28, bf16[64,32,128]{2,0,1:T(8,128)(2,1)S(1)} %all-to-all-done.3, f32[2048]{0:T(1024)S(1)} %copy-done.14, ...), kind=kLoop, calls=%fused_computation.62 | loop fusion | flops 4456448 | bytes 5251072 | tf_op jit(solution)/shard_map/convert_element_type | solution.py:164
  274.0 2.0 copy.43
  276.0 2.0 copy.44
  278.1 1.0 copy.45
  (46 shorter events, 2.3 us)
Async XLA Ops:
  0.6 2.9 %copy-start.12 = (bf16[1,128,2048]{2,1,0:T(8,128)(2,1)S(1)}, bf16[1,128,2048]{2,1,0:T(8,128)(2,1)}, u32[]{:S(2)}) copy-start(bf16[1,128,2048]{2,1,0:T(8,128)(2,1)} %param.9) | copy-start | bytes 1572868
  0.6 3.2 %copy-start.13 = (bf16[1,128,2048]{2,1,0:T(8,128)(2,1)S(1)}, bf16[1,128,2048]{2,1,0:T(8,128)(2,1)}, u32[]{:S(2)}) copy-start(bf16[1,128,2048]{2,1,0:T(8,128)(2,1)} %param.7) | copy-start | bytes 1572868
  2.1 3.4 %copy-start.5 = (bf16[1,128,2048]{1,2,0:T(8,128)(2,1)}, bf16[1,128,2048]{1,2,0:T(8,128)(2,1)S(1)}, u32[]{:S(2)}) copy-start(bf16[1,128,2048]{1,2,0:T(8,128)(2,1)S(1)} %copy.35) | copy-start | bytes 1572868
  3.6 1.9 copy-start.7
  3.9 1.6 copy-start.9
  5.5 85.1 %all-to-all-start.1 = ((bf16[32,64,128]{2,1,0:T(8,128)(2,1)}), bf16[32,64,128]{2,1,0:T(8,128)(2,1)S(1)}, u32[]{:S(2)}, u32[]{:S(2)}) async-start(bf16[32,64,128]{2,1,0:T(8,128)(2,1)} %bitcast.6), calls=%async_computation.1 | async-start | bytes 1048576 | tf_op jit(solution)/shard_map/all_to_all | solution.py:127
  90.6 32.5 %all-to-all-start = ((bf16[32,64,128]{2,1,0:T(8,128)(2,1)}), bf16[32,64,128]{2,1,0:T(8,128)(2,1)S(1)}, u32[]{:S(2)}, u32[]{:S(2)}) async-start(bf16[32,64,128]{2,1,0:T(8,128)(2,1)} %bitcast.2), calls=%async_computation | async-start | bytes 1048576 | tf_op jit(solution)/shard_map/all_to_all | solution.py:126
  123.4 2.2 copy-start.2
  130.9 3.3 %copy-start = (f32[64,64,256]{2,1,0:T(8,128)}, f32[64,64,256]{2,1,0:T(8,128)S(1)}, u32[]{:S(2)}) copy-start(f32[64,64,256]{2,1,0:T(8,128)S(1)} %fusion) | copy-start | bytes 12582916
  142.9 4.3 %copy-start.1 = (f32[64,64,256]{2,1,0:T(8,128)S(1)}, f32[64,64,256]{2,1,0:T(8,128)}, u32[]{:S(2)}) copy-start(f32[64,64,256]{2,1,0:T(8,128)} %copy-done) | copy-start | bytes 12582916
  142.9 4.3 %copy-start.3 = (f32[64,63,128]{2,1,0:T(8,128)S(1)}, f32[64,63,128]{2,1,0:T(8,128)}, u32[]{:S(2)}) copy-start(f32[64,63,128]{2,1,0:T(8,128)} %slice.122) | copy-start | bytes 6193156
  160.4 2.0 copy-start.4
  163.8 7.6 %copy-start.11 = (f32[1,64,4096]{2,1,0:T(8,128)S(1)}, f32[1,64,4096]{2,1,0:T(8,128)}, u32[]{:S(2)}) copy-start(f32[1,64,4096]{2,1,0:T(8,128)} %iota_multiply_fusion) | copy-start | bytes 3145732
  164.9 22.6 %all-to-all-start.2 = ((bf16[64,32,128]{2,0,1:T(8,128)(2,1)}), bf16[64,32,128]{2,0,1:T(8,128)(2,1)S(1)}, u32[]{:S(2)}, u32[]{:S(2)}) async-start(bf16[64,32,128]{2,0,1:T(8,128)(2,1)} %copy.41), calls=%async_computation.2 | async-start | bytes 1048576 | tf_op jit(solution)/shard_map/all_to_all | solution.py:139
  172.5 98.6 %copy-start.6 = (bf16[1,128,2048]{1,2,0:T(8,128)(2,1)S(1)}, bf16[1,128,2048]{1,2,0:T(8,128)(2,1)}, u32[]{:S(2)}) copy-start(bf16[1,128,2048]{1,2,0:T(8,128)(2,1)} %copy-done.5) | copy-start | bytes 1572868
  172.5 98.6 %copy-start.8 = (bf16[1,128,2048]{1,2,0:T(8,128)(2,1)S(1)}, bf16[1,128,2048]{1,2,0:T(8,128)(2,1)}, u32[]{:S(2)}) copy-start(bf16[1,128,2048]{1,2,0:T(8,128)(2,1)} %copy-done.7) | copy-start | bytes 1572868
  172.5 98.6 %copy-start.10 = (bf16[1,128,2048]{1,2,0:T(8,128)(2,1)S(1)}, bf16[1,128,2048]{1,2,0:T(8,128)(2,1)}, u32[]{:S(2)}) copy-start(bf16[1,128,2048]{1,2,0:T(8,128)(2,1)} %copy-done.9) | copy-start | bytes 1572868
  172.5 98.6 %copy-start.14 = (f32[2048]{0:T(1024)S(1)}, f32[2048]{0:T(1024)}, u32[]{:S(2)}) copy-start(f32[2048]{0:T(1024)} %param.13) | copy-start | bytes 24580
  187.5 83.7 %all-to-all-start.3 = ((bf16[64,32,128]{2,0,1:T(8,128)(2,1)}), bf16[64,32,128]{2,0,1:T(8,128)(2,1)S(1)}, u32[]{:S(2)}, u32[]{:S(2)}) async-start(bf16[64,32,128]{2,0,1:T(8,128)(2,1)} %copy.42), calls=%async_computation.3 | async-start | bytes 1048576 | tf_op jit(solution)/shard_map/all_to_all | solution.py:142
where the time goes:
time: 280 us; the launch traced here: 279 us
  blocking collectives  139 us (50%)
  starting transfers between devices  39.4 us (14%)
  other arithmetic  35.7 us (13%)
  local copies, waits for them, and re-layouts  27.8 us (10%)
  matrix products  18.7 us (7%)
  waiting for transfers between devices  16.6 us (6%)
    psum x1, blocking collectives, shards(): lax.psum((res_part, log_part, skip_local), 'dp')  74.3 us
    unnamed x1, blocking collectives  64.8 us
    all_to_all x1, starting transfers between devices, shards(): lax.all_to_all(prod_send, 'seq', split_axis=0, concat_axis=1, tiled=True)  15.8 us
    unnamed x40, local copies, waits for them, and re-layouts  11.8 us
    all_to_all x1, waiting for transfers between devices, shards(): lax.all_to_all(prod_send, 'seq', split_axis=0, concat_axis=1, tiled=True)  11.5 us
    all_to_all x1, starting transfers between devices, shards(): lax.all_to_all(carr_send, 'seq', split_axis=0, concat_axis=1, tiled=True)  10.2 us
    reduce_sum x1, other arithmetic, shards(): jnp.sum(jnp.exp(-decay_own[None, :, :, None] * steps_f[None, None, None,...  9.83 us
    slice x2, local copies, waits for them, and re-layouts, mirrored(): flip_d[:, 1:]  7.95 us
  transfers between devices with their start and end apart: 4, of which 2 were waited for; matrix products, arithmetic and copies ran while one was open for 10% of the time, Pallas kernels for 0%

commit v1 on v0

v1 whole, which is shorter than its diff:
```python
import functools

import jax
import jax.numpy as jnp
import ml_dtypes
import numpy as np
from jax import lax
from jax.experimental import pallas as pl
from jax.experimental.pallas import tpu as pltpu
from jax.sharding import PartitionSpec as P

MESH = pl.DeviceIdType.MESH
f32 = jnp.float32
bf16 = jnp.bfloat16


def split_table(table):
    high = table.astype(ml_dtypes.bfloat16)
    low = (table - high.astype(np.float64)).astype(ml_dtypes.bfloat16)
    return high, low


def dft_tables(rows):
    odd = 2 * np.arange(rows)[:, None] + 1
    angle = np.pi / (2 * rows) * (odd * np.arange(rows)[None, :] % (4 * rows))
    forward = np.concatenate([np.cos(angle), -np.sin(angle)], axis=0)
    inverse = np.concatenate([np.cos(angle).T, -np.sin(angle).T], axis=1) / rows
    fwd = np.concatenate(split_table(forward), axis=1)
    inv = np.concatenate(split_table(inverse), axis=0)
    return fwd, inv


def main_kernel(
    rows,
    channels,
    groups,
    batch,
    q_hbm,
    k_hbm,
    v_hbm,
    o_hbm,
    res_ref,
    rates_ref,
    gain_ref,
    fwd_ref,
    inv_ref,
    y_hbm,
    dz_hbm,
    grad_ref,
    q_in,
    k_in,
    v_in,
    o_in,
    prod2,
    carr2,
    prod_f,
    carr_f,
    prod_w,
    carr_w,
    conv_s,
    back_s,
    lag_s,
    lag_w,
    up_tab,
    down_tab,
    gam_one,
    gam_eight,
    coef_t,
    coef_h,
    coef_k,
    y_out,
    dz_out,
    send_a,
    recv_a,
    send_b,
    recv_b,
    send_l,
    recv_l,
    send_g,
    recv_g,
    in_sem,
    out_sem,
    a_send,
    a_recv,
    b_send,
    b_recv,
    l_send,
    l_recv,
    g_send,
    g_recv,
):
    length = rows * groups
    inv_len = 1.0 / length
    wide = min(512, channels)
    mid = min(256, channels)
    chunks = channels // wide
    per_chunk = groups // chunks
    me = lax.axis_index("seq")
    me_b = lax.axis_index("dp")

    def seq_peer(step):
        return lax.rem(me + step, groups)

    def dp_peer(step):
        return lax.rem(me_b + step, batch)

    def lanes_of(index, size):
        return pl.ds(pl.multiple_of(index * size, size), size)

    def chunk_at(step):
        return lax.rem(me // per_chunk + step, chunks)

    def in_copies(step):
        lanes = lanes_of(chunk_at(step), wide)
        return [
            pltpu.make_async_copy(src.at[:, lanes], dst.at[:, lanes], in_sem.at[which, step])
            for which, (src, dst) in enumerate(
                ((k_hbm, k_in), (v_hbm, v_in), (o_hbm, o_in), (q_hbm, q_in))
            )
        ]

    for step in range(chunks):
        for copy in in_copies(step):
            copy.start()

    barrier = pltpu.get_barrier_semaphore()

    def greet_seq(step, _):
        pl.semaphore_signal(barrier, inc=1, device_id={"seq": seq_peer(step)}, device_id_type=MESH)
        return 0

    def greet_dp(step, _):
        pl.semaphore_signal(barrier, inc=1, device_id={"dp": dp_peer(step)}, device_id_type=MESH)
        return 0

    lax.fori_loop(1, groups, greet_seq, 0)
    lax.fori_loop(1, batch, greet_dp, 0)

    decay_all = rates_ref[...] * inv_len
    gam_one[...] = jnp.exp(-decay_all)
    sub = lax.broadcasted_iota(jnp.int32, (8, channels), 0).astype(f32)

    def table_body(n, _):
        rate = rates_ref[pl.ds(n, 1), :] * inv_len
        gam_eight[n] = jnp.exp(-8.0 * rate)
        coef_t[n] = res_ref[pl.ds(n, 1), :]
        up_tab[n] = jnp.exp(-rate * sub)
        down_tab[n] = jnp.exp(-rate * (8.0 - sub))
        return 0

    lax.fori_loop(0, 16, table_body, 0)

    lane = lax.broadcasted_iota(jnp.int32, (8, 128), 1)
    left = lane < 64

    def pack(block):
        top = block[0:8]
        low = block[8:16]
        return (
            jnp.where(left, top, pltpu.roll(low, 64, 1)),
            jnp.where(left, pltpu.roll(top, 64, 1), low),
        )

    def horner(up_refs, down_refs, lanes, width):
        gamma = gam_one[:, lanes]
        zero = jnp.zeros((16, width), f32)
        ups = len(up_refs)

        def body(i, carry):
            ups_in = [ref[pl.ds(pl.multiple_of(i * 8, 8), 8), lanes] for ref in up_refs]
            base = pl.multiple_of(rows - 8 - i * 8, 8)
            downs_in = [ref[pl.ds(base, 8), lanes] for ref in down_refs]
            totals = list(carry)
            for r in range(8):
                for which, block in enumerate(ups_in):
                    totals[which] = totals[which] * gamma + block[r : r + 1]
                for which, block in enumerate(downs_in):
                    totals[ups + which] = totals[ups + which] * gamma + block[7 - r : 8 - r]
            return tuple(totals)

        count = ups + len(down_refs)
        totals = lax.fori_loop(0, rows // 8, body, (zero,) * count, unroll=2)
        return [t * gamma for t in totals[:ups]] + list(totals[ups:])

    def send_a_copy(owner):
        return pltpu.make_async_remote_copy(
            src_ref=send_a.at[owner],
            dst_ref=recv_a.at[me],
            send_sem=a_send,
            recv_sem=a_recv,
            device_id={"seq": owner},
            device_id_type=MESH,
        )

    down_weight = (rows - lax.broadcasted_iota(jnp.int32, (rows, wide), 0)).astype(f32)
    up_weight = lax.broadcasted_iota(jnp.int32, (rows, wide), 0).astype(f32)

    for step in range(chunks):
        chunk = chunk_at(step)
        lanes = lanes_of(chunk, wide)
        for copy in in_copies(step):
            copy.wait()
        prod = (k_in[:, lanes].astype(f32) * v_in[:, lanes].astype(f32)).astype(bf16)
        carr = (o_in[:, lanes].astype(f32) * q_in[:, lanes].astype(f32)).astype(bf16)
        prod2[0:rows, lanes] = prod
        prod2[rows : 2 * rows, lanes] = prod
        carr2[0:rows, lanes] = carr
        carr2[rows : 2 * rows, lanes] = carr
        prod_32 = prod.astype(f32)
        carr_32 = carr.astype(f32)
        prod_f[:, lanes] = prod_32
        carr_f[:, lanes] = carr_32
        prod_w[:, lanes] = prod_32 * down_weight
        carr_w[:, lanes] = carr_32 * up_weight
        skip = jnp.sum(prod_32 * carr_32, axis=0, keepdims=True)
        state_p, state_c = horner([prod_f], [carr_f], lanes, wide)
        for part in range(wide // 128):
            cut = slice(part * 128, part * 128 + 128)
            pair = chunk * (wide // 128) + part
            for half, (p_tile, c_tile) in enumerate(zip(pack(state_p[:, cut]), pack(state_c[:, cut]))):
                send_a[2 * pair + half, 0:8, :] = p_tile
                send_a[2 * pair + half, 8:16, :] = c_tile
            row = skip[:, cut]
            send_a[2 * pair, 16:17, :] = row
            send_a[2 * pair + 1, 16:17, :] = pltpu.roll(row, 64, 1)
        if step == 0:
            pl.semaphore_wait(barrier, groups - 1 + batch - 1)

        def send_body(i, _):
            owner = chunk * per_chunk + lax.rem(me + i, per_chunk)

            @pl.when(owner != me)
            def _():
                send_a_copy(owner).start()

            return 0

        lax.fori_loop(0, per_chunk, send_body, 0)
    recv_a[me] = send_a[me]

    def synth(coef_ref, table_ref, lanes, width, ascending):
        def body(n, accs):
            accs = list(accs)
            wave = table_ref[n, :, lanes] * coef_ref[n, :, lanes]
            ratio = jnp.broadcast_to(gam_eight[n, :, lanes], (8, width))
            blocks = range(rows // 8) if ascending else range(rows // 8 - 1, -1, -1)
            for order, block in enumerate(blocks):
                accs[block] = accs[block] + wave
                if order < rows // 8 - 1:
                    wave = wave * ratio
            return tuple(accs)

        zero = jnp.zeros((8, width), f32)
        accs = lax.fori_loop(0, 16, body, (zero,) * (rows // 8), unroll=2)
        return jnp.concatenate(accs, axis=0)

    def dot(a, b):
        return jnp.dot(a, b, preferred_element_type=f32)

    def spectrum_body(j, _):
        lanes = lanes_of(j, mid)
        taps = synth(coef_t, up_tab, lanes, mid, True)
        high = taps.astype(bf16)
        low = (taps - high.astype(f32)).astype(bf16)
        table = fwd_ref[...]
        filt = dot(table, jnp.concatenate([high, high], axis=0)) + dot(table[:, :rows], low)
        spec_p = dot(table, prod2[:, lanes])
        spec_c = dot(table, carr2[:, lanes])
        fr, fi = filt[:rows], filt[rows:]
        pr, pi = spec_p[:rows], spec_p[rows:]
        cr, ci = spec_c[:rows], spec_c[rows:]
        inverse = inv_ref[...]

        def back_to_rows(real, imag):
            spec = jnp.concatenate([real.astype(bf16), imag.astype(bf16)], axis=0)
            both = dot(inverse, spec)
            return both[:rows] + both[rows:]

        conv_s[:, lanes] = back_to_rows(pr * fr - pi * fi, pr * fi + pi * fr)
        back_s[:, lanes] = back_to_rows(cr * fr + ci * fi, ci * fr - cr * fi)
        lag = back_to_rows(cr * pr + ci * pi, ci * pr - cr * pi)
        lag_s[:, lanes] = lag
        lag_w[:, lanes] = lag * up_weight[:, :mid]
        return 0

    lax.fori_loop(0, channels // mid, spectrum_body, 0)

    def wait_bytes(ref, sem, count):
        block = ref.at[pl.ds(0, count)]
        pltpu.make_async_copy(block, block, sem).wait()

    wait_bytes(recv_a, a_recv, groups - 1)
    own_lanes = lanes_of(me // 2, 128)
    is_left = lax.rem(me, 2) == 0

    def own_pack(block):
        first, second = pack(block)
        return jnp.where(is_left, first, second)

    own_decay = own_pack(rates_ref[:, own_lanes]) * inv_len
    own_res = own_pack(res_ref[:, own_lanes])
    span = jnp.exp(-own_decay * float(rows))
    zero = jnp.zeros((8, 128), f32)

    def up_scan(i, carry):
        state, slope, total, moment = carry
        p_in = recv_a[i, 0:8, :]
        c_in = recv_a[i, 8:16, :]
        send_b[i, 0:8, :] = state
        total = total + c_in * state
        moment = moment + c_in * slope
        slope = span * (slope + state)
        state = span * state + p_in
        return state, slope, total, moment

    _, _, total, moment = lax.fori_loop(0, groups, up_scan, (zero, zero, zero, zero), unroll=4)

    def down_scan(i, state):
        at = groups - 1 - i
        send_b[at, 8:16, :] = state
        return span * state + recv_a[at, 8:16, :]

    lax.fori_loop(0, groups, down_scan, zero, unroll=4)

    def send_b_body(step, _):
        owner = seq_peer(step)
        pltpu.make_async_remote_copy(
            src_ref=send_b.at[owner],
            dst_ref=recv_b.at[me],
            send_sem=b_send,
            recv_sem=b_recv,
            device_id={"seq": owner},
            device_id_type=MESH,
        ).start()
        return 0

    lax.fori_loop(1, groups, send_b_body, 0)
    recv_b[me] = send_b[me]

    def skip_body(i, acc):
        return acc + recv_a[i, 16:17, :]

    skip_sum = lax.fori_loop(0, groups, skip_body, jnp.zeros((1, 128), f32))

    def moments_body(j, _):
        lanes = lanes_of(j, mid)
        slope_p, slope_c, lag_0, lag_1 = horner([prod_w], [carr_w, lag_s, lag_w], lanes, mid)
        for part in range(mid // 128):
            cut = slice(part * 128, part * 128 + 128)
            pair = j * (mid // 128) + part
            tiles = [pack(x[:, cut]) for x in (slope_p, slope_c, lag_0, lag_1)]
            for half in range(2):
                send_l[2 * pair + half, 0] = jnp.concatenate(
                    [tiles[0][half], tiles[1][half]], axis=0
                ).astype(bf16)
                send_l[2 * pair + half, 1] = jnp.concatenate(
                    [tiles[2][half], tiles[3][half]], axis=0
                ).astype(bf16)
        return 0

    lax.fori_loop(0, channels // mid, moments_body, 0)

    def send_l_body(step, _):
        owner = seq_peer(step)
        pltpu.make_async_remote_copy(
            src_ref=send_l.at[owner],
            dst_ref=recv_l.at[me],
            send_sem=l_send,
            recv_sem=l_recv,
            device_id={"seq": owner},
            device_id_type=MESH,
        ).start()
        return 0

    lax.fori_loop(1, groups, send_l_body, 0)
    recv_l[me] = send_l[me]

    wait_bytes(recv_b, b_recv, groups - 1)

    def unpack_body(j, _):
        lanes = lanes_of(j, 128)
        res = res_ref[:, lanes]
        for half, coef in ((0, coef_h), (8, coef_k)):
            first = recv_b[2 * j, half : half + 8, :]
            second = recv_b[2 * j + 1, half : half + 8, :]
            low = res[0:8] * jnp.where(left, first, pltpu.roll(second, 64, 1))
            high = res[8:16] * jnp.where(left, pltpu.roll(first, 64, 1), second)
            for row in range(8):
                coef[row, :, lanes] = low[row : row + 1]
                coef[row + 8, :, lanes] = high[row : row + 1]
        return 0

    lax.fori_loop(0, channels // 128, unpack_body, 0)

    def out_copies(j):
        lanes = lanes_of(j, mid)
        return [
            pltpu.make_async_copy(src.at[:, lanes], dst.at[:, lanes], out_sem.at[which])
            for which, (src, dst) in enumerate(((y_out, y_hbm), (dz_out, dz_hbm)))
        ]

    def final_body(j, _):
        for part in range(mid // 128):
            lanes = lanes_of(j * (mid // 128) + part, 128)
            conv = conv_s[:, lanes] + synth(coef_h, up_tab, lanes, 128, True)
            back = back_s[:, lanes] + synth(coef_k, down_tab, lanes, 128, False)
            gain = gain_ref[:, lanes]
            y_out[:, lanes] = conv.astype(bf16).astype(f32) + gain * prod_f[:, lanes]
            dz_out[:, lanes] = back.astype(bf16).astype(f32) + gain * carr_f[:, lanes]
        for copy in out_copies(j):
            copy.start()
        return 0

    steps = channels // mid
    early = steps // 2
    lax.fori_loop(0, early, final_body, 0)

    wait_bytes(recv_l, l_recv, groups - 1)

    def combine_body(i, carry):
        grad_0, grad_1 = carry
        slopes = recv_l[i, 0].astype(f32)
        lags = recv_l[i, 1].astype(f32)
        grad_0 = grad_0 + lags[0:8]
        grad_1 = grad_1 + lags[8:16]
        grad_1 = grad_1 + slopes[8:16] * send_b[i, 0:8, :] + slopes[0:8] * send_b[i, 8:16, :]
        return grad_0, grad_1

    grad_0, grad_1 = lax.fori_loop(
        0, groups, combine_body, (total, float(rows) * moment), unroll=4
    )
    send_g[0:8, :] = grad_0 * inv_len
    send_g[8:16, :] = -own_res * own_decay * grad_1 * inv_len
    send_g[16:17, :] = skip_sum * inv_len

    def send_g_body(step, _):
        pltpu.make_async_remote_copy(
            src_ref=send_g,
            dst_ref=recv_g.at[me_b],
            send_sem=g_send,
            recv_sem=g_recv,
            device_id={"dp": dp_peer(step)},
            device_id_type=MESH,
        ).start()
        return 0

    lax.fori_loop(1, batch, send_g_body, 0)
    recv_g[me_b] = send_g[...]
    lax.fori_loop(early, steps, final_body, 0)
    wait_bytes(recv_g, g_recv, batch - 1)

    def total_body(i, acc):
        return acc + recv_g[i]

    grad_ref[0:17, :] = lax.fori_loop(0, batch, total_body, jnp.zeros((17, 128), f32))

    wait_bytes(send_a, a_send, groups - 1)
    wait_bytes(send_b, b_send, groups - 1)
    wait_bytes(send_l, l_send, groups - 1)
    wait_bytes(recv_g, g_send, batch - 1)

    def drain(j, _):
        for copy in out_copies(j):
            copy.wait()
        return 0

    lax.fori_loop(0, steps, drain, 0)


def gate_kernel(cot, key, value, y, dz, grads, grad_q, grad_k, grad_v, grad_r, grad_l, grad_s):
    dz_now = dz[...]
    grad_q[...] = (cot[...].astype(f32) * y[...]).astype(bf16)
    grad_k[...] = (dz_now * value[...].astype(f32)).astype(bf16)
    grad_v[...] = (dz_now * key[...].astype(f32)).astype(bf16)

    @pl.when(pl.program_id(0) == 0)
    def _():
        for start, out in ((0, grad_r), (8, grad_l)):
            tile = grads[start : start + 8, :]
            out[0:8, :] = tile[:, 0:64]
            out[8:16, :] = pltpu.roll(tile, 64, 1)[:, 0:64]
        grad_s[...] = grads[16:17, 0:64]


def shards(queries, key_branch, value_branch, cotangent, residues, rates, skip_gain):
    groups = lax.axis_size("seq")
    batch = lax.axis_size("dp")
    rows, channels = queries.shape[1:]
    fwd, inv = dft_tables(rows)
    q, k, v, o = (x[0] for x in (queries, key_branch, value_branch, cotangent))
    hbm = pl.BlockSpec(memory_space=pl.ANY)
    vmem = pl.BlockSpec(memory_space=pltpu.VMEM)
    big = pltpu.VMEM((rows, channels), f32)
    half = pltpu.VMEM((rows, channels), bf16)
    dma = pltpu.SemaphoreType.DMA
    chunks = channels // min(512, channels)
    y, dz, grads = pl.pallas_call(
        functools.partial(main_kernel, rows, channels, groups, batch),
        out_shape=[
            jax.ShapeDtypeStruct((rows, channels), f32),
            jax.ShapeDtypeStruct((rows, channels), f32),
            jax.ShapeDtypeStruct((24, 128), f32),
        ],
        in_specs=[hbm] * 4 + [vmem] * 5,
        out_specs=[hbm, hbm, vmem],
        scratch_shapes=[half] * 4
        + [pltpu.VMEM((2 * rows, channels), bf16)] * 2
        + [big] * 8
        + [pltpu.VMEM((16, 8, channels), f32)] * 2
        + [pltpu.VMEM((16, channels), f32)]
        + [pltpu.VMEM((16, 1, channels), f32)] * 4
        + [big] * 2
        + [pltpu.VMEM((groups, 17, 128), f32)] * 2
        + [pltpu.VMEM((groups, 16, 128), f32)] * 2
        + [pltpu.VMEM((groups, 2, 16, 128), bf16)] * 2
        + [pltpu.VMEM((17, 128), f32), pltpu.VMEM((batch, 17, 128), f32)]
        + [dma((4, chunks)), dma((2,))]
        + [dma] * 8,
        compiler_params=pltpu.CompilerParams(
            collective_id=0, has_side_effects=True, vmem_limit_bytes=48 * 2**20
        ),
        name="hyena_main",
    )(q, k, v, o, residues, rates, skip_gain[None, :], jnp.asarray(fwd), jnp.asarray(inv))
    tile = min(32, rows)
    rowed = pl.BlockSpec((tile, channels), lambda i: (i, 0))

    def whole(*shape):
        return pl.BlockSpec(shape, lambda i: (0, 0))

    wide16 = jax.ShapeDtypeStruct((rows, channels), bf16)
    gq, gk, gv, gr, gl, gs = pl.pallas_call(
        gate_kernel,
        grid=(rows // tile,),
        out_shape=[wide16] * 3
        + [jax.ShapeDtypeStruct((16, 64), f32)] * 2
        + [jax.ShapeDtypeStruct((1, 64), f32)],
        in_specs=[rowed] * 5 + [whole(24, 128)],
        out_specs=[rowed] * 3 + [whole(16, 64), whole(16, 64), whole(1, 64)],
        name="hyena_gate",
    )(o, k, v, y, dz, grads)
    return gq[None], gk[None], gv[None], gr, gl, gs[0]


def solution(mesh):
    row_spec = P("dp", "seq", None)
    return jax.shard_map(
        shards,
        mesh=mesh,
        in_specs=(row_spec,) * 4 + (P(),) * 3,
        out_specs=(row_spec,) * 3 + (P(None, "seq"), P(None, "seq"), P("seq")),
        check_vma=False,
    )
```

time: 280 us -> 64.4 us (0.23)
  the two profiles are of different devices: /device:TPU:6 before, /device:TPU:1 now
where the time goes in v1:
time: 64.4 us; the launch traced here: 63.9 us
  Pallas kernels  52.2 us (81%)
  local copies, waits for them, and re-layouts  11 us (17%)
  between operations  0.67 us (1%)
    pallas_call x1, Pallas kernels, shards(): pl.pallas_call(functools.partial(main_kernel, rows, channels, groups, bat...  48.1 us
    unnamed x24, local copies, waits for them, and re-layouts  11 us
    pallas_call x1, Pallas kernels, shards(): pl.pallas_call(gate_kernel, grid=(rows // tile,), out_shape=[wide16] * 3...  4.1 us

profile of v1, /device:TPU:1, one launch (start us, length us, event | category | flops | bytes accessed | tf_op | source)
XLA Modules:
  0.0 63.9 jit_solution(16338953248390201044)
XLA Ops:
  0.6 0.0 copy-start.11
  0.6 0.7 %copy-done.11 = f32[2048]{0:T(1024)S(1)} copy-done((f32[2048]{0:T(1024)S(1)}, f32[2048]{0:T(1024)}, u32[]{:S(2)}) %copy-start.11) | copy-done | bytes 8216
  1.3 0.0 copy-start
  1.3 1.0 %copy-done = bf16[1,128,2048]{2,1,0:T(8,128)(2,1)S(1)} copy-done((bf16[1,128,2048]{2,1,0:T(8,128)(2,1)S(1)}, bf16[1,128,2048]{2,1,0:T(8,128)(2,1)}, u32[]{:S(2)}) %copy-start) | copy-done | bytes 524312
  2.4 0.0 copy-start.1
  2.4 1.0 %copy-done.1 = bf16[1,128,2048]{2,1,0:T(8,128)(2,1)S(1)} copy-done((bf16[1,128,2048]{2,1,0:T(8,128)(2,1)S(1)}, bf16[1,128,2048]{2,1,0:T(8,128)(2,1)}, u32[]{:S(2)}) %copy-start.1) | copy-done | bytes 524312
  3.4 0.0 copy-start.2
  3.4 1.0 %copy-done.2 = bf16[1,128,2048]{2,1,0:T(8,128)(2,1)S(1)} copy-done((bf16[1,128,2048]{2,1,0:T(8,128)(2,1)S(1)}, bf16[1,128,2048]{2,1,0:T(8,128)(2,1)}, u32[]{:S(2)}) %copy-start.2) | copy-done | bytes 524312
  4.5 0.0 copy-start.5
  4.5 1.0 %copy-done.5 = bf16[1,128,2048]{2,1,0:T(8,128)(2,1)S(1)} copy-done((bf16[1,128,2048]{2,1,0:T(8,128)(2,1)S(1)}, bf16[1,128,2048]{2,1,0:T(8,128)(2,1)}, u32[]{:S(2)}) %copy-start.5) | copy-done | bytes 524312
  5.5 0.0 copy-start.6
  5.5 0.9 %copy-done.6 = f32[16,2048]{1,0:T(8,128)S(1)} copy-done((f32[16,2048]{1,0:T(8,128)S(1)}, f32[16,2048]{1,0:T(8,128)}, u32[]{:S(2)}) %copy-start.6) | copy-done | bytes 131096
  6.4 0.0 copy-start.7
  6.4 0.9 %copy-done.7 = f32[16,2048]{1,0:T(8,128)S(1)} copy-done((f32[16,2048]{1,0:T(8,128)S(1)}, f32[16,2048]{1,0:T(8,128)}, u32[]{:S(2)}) %copy-start.7) | copy-done | bytes 131096
  7.3 0.0 copy-start.8
  7.3 0.9 %copy-done.8 = bf16[256,256]{1,0:T(8,128)(2,1)S(1)} copy-done((bf16[256,256]{1,0:T(8,128)(2,1)S(1)}, bf16[256,256]{1,0:T(8,128)(2,1)}, u32[]{:S(2)}) %copy-start.8) | copy-done | bytes 131096
  8.2 0.0 copy-start.9
  8.2 0.9 %copy-done.9 = bf16[256,256]{1,0:T(8,128)(2,1)S(1)} copy-done((bf16[256,256]{1,0:T(8,128)(2,1)S(1)}, bf16[256,256]{1,0:T(8,128)(2,1)}, u32[]{:S(2)}) %copy-start.9) | copy-done | bytes 131096
  9.1 48.1 %hyena_main.1 = (f32[128,2048]{1,0:T(8,128)S(1)}, f32[128,2048]{1,0:T(8,128)S(1)}, f32[24,128]{1,0:T(8,128)S(1)}) custom-call(bf16[128,2048]{1,0:T(8,128)(2,1)S(1)} %bitcast.15, bf16[128,2048]{1,0:T(8,128)(2,1)S(1)} %bitcast.12, bf16[128,2048]{1,0:T(8,128)(2,1)S(1)} %bitcast.14, bf16[128,2048]{1,0:T(8,128)(2,1)S(1)} %bitcast.10, f32[16,2048]{1,0:T(8,128)S(1)} %copy-done.6, ...), custom_call_target="tpu_custom_call" | custom-call | tf_op jit(solution)/shard_map/hyena_main/pallas_call | solution.py:497
  57.2 0.0 copy-start.3
  57.2 1.0 %copy-done.3 = f32[128,2048]{1,0:T(8,128)} copy-done((f32[128,2048]{1,0:T(8,128)}, f32[128,2048]{1,0:T(8,128)S(1)}, u32[]{:S(2)}) %copy-start.3) | copy-done | bytes 1048600
  58.2 0.0 copy-start.4
  58.2 1.0 %copy-done.4 = f32[128,2048]{1,0:T(8,128)} copy-done((f32[128,2048]{1,0:T(8,128)}, f32[128,2048]{1,0:T(8,128)S(1)}, u32[]{:S(2)}) %copy-start.4) | copy-done | bytes 1048600
  59.2 0.0 copy-start.10
  59.2 0.6 copy-done.10
  59.8 4.1 %hyena_gate.1 = (bf16[128,2048]{1,0:T(8,128)(2,1)}, bf16[128,2048]{1,0:T(8,128)(2,1)}, bf16[128,2048]{1,0:T(8,128)(2,1)}, f32[16,64]{1,0:T(8,128)}, f32[16,64]{1,0:T(8,128)}, /*index=5*/f32[1,64]{1,0:T(1,128)}) custom-call(bf16[128,2048]{1,0:T(8,128)(2,1)} %bitcast.9, bf16[128,2048]{1,0:T(8,128)(2,1)} %bitcast.11, bf16[128,2048]{1,0:T(8,128)(2,1)} %bitcast.13, ...), custom_call_target="tpu_custom_call" | custom-call | tf_op jit(solution)/shard_map/hyena_gate/pallas_call | solution.py:531
Async XLA Ops:
  0.6 0.7 %copy-start.11 = (f32[2048]{0:T(1024)S(1)}, f32[2048]{0:T(1024)}, u32[]{:S(2)}) copy-start(f32[2048]{0:T(1024)} %param.15) | copy-start | bytes 24580
  1.3 1.0 %copy-start = (bf16[1,128,2048]{2,1,0:T(8,128)(2,1)S(1)}, bf16[1,128,2048]{2,1,0:T(8,128)(2,1)}, u32[]{:S(2)}) copy-start(bf16[1,128,2048]{2,1,0:T(8,128)(2,1)} %param.12) | copy-start | bytes 1572868
  2.4 1.0 %copy-start.1 = (bf16[1,128,2048]{2,1,0:T(8,128)(2,1)S(1)}, bf16[1,128,2048]{2,1,0:T(8,128)(2,1)}, u32[]{:S(2)}) copy-start(bf16[1,128,2048]{2,1,0:T(8,128)(2,1)} %param.10) | copy-start | bytes 1572868
  3.4 1.0 %copy-start.2 = (bf16[1,128,2048]{2,1,0:T(8,128)(2,1)S(1)}, bf16[1,128,2048]{2,1,0:T(8,128)(2,1)}, u32[]{:S(2)}) copy-start(bf16[1,128,2048]{2,1,0:T(8,128)(2,1)} %param.11) | copy-start | bytes 1572868
  4.5 1.0 %copy-start.5 = (bf16[1,128,2048]{2,1,0:T(8,128)(2,1)S(1)}, bf16[1,128,2048]{2,1,0:T(8,128)(2,1)}, u32[]{:S(2)}) copy-start(bf16[1,128,2048]{2,1,0:T(8,128)(2,1)} %param.9) | copy-start | bytes 1572868
  5.5 0.9 %copy-start.6 = (f32[16,2048]{1,0:T(8,128)S(1)}, f32[16,2048]{1,0:T(8,128)}, u32[]{:S(2)}) copy-start(f32[16,2048]{1,0:T(8,128)} %res_ref.1) | copy-start | bytes 393220
  6.4 0.9 %copy-start.7 = (f32[16,2048]{1,0:T(8,128)S(1)}, f32[16,2048]{1,0:T(8,128)}, u32[]{:S(2)}) copy-start(f32[16,2048]{1,0:T(8,128)} %rates_ref.1) | copy-start | bytes 393220
  7.3 0.9 %copy-start.8 = (bf16[256,256]{1,0:T(8,128)(2,1)S(1)}, bf16[256,256]{1,0:T(8,128)(2,1)}, u32[]{:S(2)}) copy-start(bf16[256,256]{1,0:T(8,128)(2,1)} %constant.5.clone.inv_ref) | copy-start | bytes 393220
  8.2 0.9 %copy-start.9 = (bf16[256,256]{1,0:T(8,128)(2,1)S(1)}, bf16[256,256]{1,0:T(8,128)(2,1)}, u32[]{:S(2)}) copy-start(bf16[256,256]{1,0:T(8,128)(2,1)} %constant.4.clone.fwd_ref) | copy-start | bytes 393220
  57.2 1.0 %copy-start.3 = (f32[128,2048]{1,0:T(8,128)}, f32[128,2048]{1,0:T(8,128)S(1)}, u32[]{:S(2)}) copy-start(f32[128,2048]{1,0:T(8,128)S(1)} %get-tuple-element.15.y) | copy-start | bytes 3145732
  58.2 1.0 %copy-start.4 = (f32[128,2048]{1,0:T(8,128)}, f32[128,2048]{1,0:T(8,128)S(1)}, u32[]{:S(2)}) copy-start(f32[128,2048]{1,0:T(8,128)S(1)} %get-tuple-element.16.dz) | copy-start | bytes 3145732
  59.2 0.6 copy-start.10

commit v2 on v1

--- a/solution.py
+++ b/solution.py
@@ -25,9 +25,22 @@
     angle = np.pi / (2 * rows) * (odd * np.arange(rows)[None, :] % (4 * rows))
     forward = np.concatenate([np.cos(angle), -np.sin(angle)], axis=0)
     inverse = np.concatenate([np.cos(angle).T, -np.sin(angle).T], axis=1) / rows
+    return forward, inverse
+
+
+def stacked_tables(rows, sub_rows):
+    forward, inverse = dft_tables(rows)
+    sub_fwd, sub_inv = dft_tables(sub_rows)
+    parts = rows // sub_rows
+    blocks = np.zeros((2, sub_rows, parts, parts, sub_rows))
+    for part in range(parts):
+        blocks[:, :, part, part, :] = sub_fwd.reshape(2, sub_rows, sub_rows)
+    blocks = blocks.transpose(0, 2, 1, 3, 4).reshape(2 * rows, rows)
     fwd = np.concatenate(split_table(forward), axis=1)
     inv = np.concatenate(split_table(inverse), axis=0)
-    return fwd, inv
+    fwd_sub = np.concatenate(split_table(blocks), axis=1)
+    inv_sub = np.concatenate(split_table(sub_inv), axis=0)
+    return fwd, inv, fwd_sub, inv_sub
 
 
 def main_kernel(
@@ -39,14 +52,23 @@
     k_hbm,
     v_hbm,
     o_hbm,
+    res_hbm,
+    rates_hbm,
+    gain_hbm,
+    fwd_hbm,
+    inv_hbm,
+    fsub_hbm,
+    isub_hbm,
+    y_hbm,
+    dz_hbm,
+    grad_ref,
     res_ref,
     rates_ref,
     gain_ref,
     fwd_ref,
     inv_ref,
-    y_hbm,
-    dz_hbm,
-    grad_ref,
+    fsub_ref,
+    isub_ref,
     q_in,
     k_in,
     v_in,
@@ -64,6 +86,11 @@
     up_tab,
     down_tab,
     gam_one,
+    gam_sub,
+    sub_s,
+    sub_b,
+    sub_s1,
+    sub_b1,
     gam_eight,
     coef_t,
     coef_h,
@@ -79,6 +106,7 @@
     send_g,
     recv_g,
     in_sem,
+    small_sem,
     out_sem,
     a_send,
     a_recv,
@@ -91,6 +119,8 @@
 ):
     length = rows * groups
     inv_len = 1.0 / length
+    sub_rows = isub_ref.shape[0] // 2
+    parts = rows // sub_rows
     wide = min(512, channels)
     mid = min(256, channels)
     chunks = channels // wide
@@ -119,9 +149,27 @@
             )
         ]
 
+    small = [
+        pltpu.make_async_copy(src, dst, small_sem.at[which])
+        for which, (src, dst) in enumerate(
+            (
+                (rates_hbm, rates_ref),
+                (res_hbm, res_ref),
+                (gain_hbm, gain_ref),
+                (fwd_hbm, fwd_ref),
+                (inv_hbm, inv_ref),
+                (fsub_hbm, fsub_ref),
+                (isub_hbm, isub_ref),
+            )
+        )
+    ]
+    for copy in small[:2]:
+        copy.start()
     for step in range(chunks):
         for copy in in_copies(step):
             copy.start()
+    for copy in small[2:]:
+        copy.start()
 
     barrier = pltpu.get_barrier_semaphore()
 
@@ -136,8 +184,11 @@
     lax.fori_loop(1, groups, greet_seq, 0)
     lax.fori_loop(1, batch, greet_dp, 0)
 
+    for copy in small[:2]:
+        copy.wait()
     decay_all = rates_ref[...] * inv_len
     gam_one[...] = jnp.exp(-decay_all)
+    gam_sub[...] = jnp.exp(-float(sub_rows) * decay_all)
     sub = lax.broadcasted_iota(jnp.int32, (8, channels), 0).astype(f32)
 
     def table_body(n, _):
@@ -161,26 +212,20 @@
             jnp.where(left, pltpu.roll(top, 64, 1), low),
         )
 
-    def horner(up_refs, down_refs, lanes, width):
+    def horner(up_refs, down_refs, base, lanes, width):
         gamma = gam_one[:, lanes]
-        zero = jnp.zeros((16, width), f32)
+        totals = [jnp.zeros((16, width), f32)] * (len(up_refs) + len(down_refs))
         ups = len(up_refs)
-
-        def body(i, carry):
-            ups_in = [ref[pl.ds(pl.multiple_of(i * 8, 8), 8), lanes] for ref in up_refs]
-            base = pl.multiple_of(rows - 8 - i * 8, 8)
-            downs_in = [ref[pl.ds(base, 8), lanes] for ref in down_refs]
-            totals = list(carry)
+        for i in range(sub_rows // 8):
+            ups_in = [ref[pl.ds(pl.multiple_of(base + i * 8, 8), 8), lanes] for ref in up_refs]
+            low = pl.multiple_of(base + sub_rows - 8 - i * 8, 8)
+            downs_in = [ref[pl.ds(low, 8), lanes] for ref in down_refs]
             for r in range(8):
                 for which, block in enumerate(ups_in):
                     totals[which] = totals[which] * gamma + block[r : r + 1]
                 for which, block in enumerate(downs_in):
                     totals[ups + which] = totals[ups + which] * gamma + block[7 - r : 8 - r]
-            return tuple(totals)
-
-        count = ups + len(down_refs)
-        totals = lax.fori_loop(0, rows // 8, body, (zero,) * count, unroll=2)
-        return [t * gamma for t in totals[:ups]] + list(totals[ups:])
+        return [t * gamma for t in totals[:ups]] + totals[ups:]
 
     def send_a_copy(owner):
         return pltpu.make_async_remote_copy(
@@ -192,8 +237,9 @@
             device_id_type=MESH,
         )
 
-    down_weight = (rows - lax.broadcasted_iota(jnp.int32, (rows, wide), 0)).astype(f32)
-    up_weight = lax.broadcasted_iota(jnp.int32, (rows, wide), 0).astype(f32)
+    local = lax.rem(lax.broadcasted_iota(jnp.int32, (rows, wide), 0), sub_rows)
+    down_weight = (sub_rows - local).astype(f32)
+    up_weight = local.astype(f32)
 
     for step in range(chunks):
         chunk = chunk_at(step)
@@ -213,7 +259,19 @@
         prod_w[:, lanes] = prod_32 * down_weight
         carr_w[:, lanes] = carr_32 * up_weight
         skip = jnp.sum(prod_32 * carr_32, axis=0, keepdims=True)
-        state_p, state_c = horner([prod_f], [carr_f], lanes, wide)
+
+        def state_body(part, _):
+            base = pl.multiple_of(part * sub_rows, sub_rows)
+            sub_s[part, :, lanes], sub_b[part, :, lanes] = horner([prod_f], [carr_f], base, lanes, wide)
+            return 0
+
+        lax.fori_loop(0, parts, state_body, 0)
+        ratio = gam_sub[:, lanes]
+        state_p = sub_s[0, :, lanes]
+        state_c = sub_b[parts - 1, :, lanes]
+        for part in range(1, parts):
+            state_p = state_p * ratio + sub_s[part, :, lanes]
+            state_c = state_c * ratio + sub_b[parts - 1 - part, :, lanes]
         for part in range(wide // 128):
             cut = slice(part * 128, part * 128 + 128)
             pair = chunk * (wide // 128) + part
@@ -238,28 +296,173 @@
         lax.fori_loop(0, per_chunk, send_body, 0)
     recv_a[me] = send_a[me]
 
-    def synth(coef_ref, table_ref, lanes, width, ascending):
+    def synth(terms, lanes):
+        count = rows // 8
+        zero = jnp.zeros((8, 128), f32)
+
         def body(n, accs):
-            accs = list(accs)
-            wave = table_ref[n, :, lanes] * coef_ref[n, :, lanes]
-            ratio = jnp.broadcast_to(gam_eight[n, :, lanes], (8, width))
-            blocks = range(rows // 8) if ascending else range(rows // 8 - 1, -1, -1)
-            for order, block in enumerate(blocks):
-                accs[block] = accs[block] + wave
-                if order < rows // 8 - 1:
-                    wave = wave * ratio
-            return tuple(accs)
-
-        zero = jnp.zeros((8, width), f32)
-        accs = lax.fori_loop(0, 16, body, (zero,) * (rows // 8), unroll=2)
-        return jnp.concatenate(accs, axis=0)
+            accs = [list(acc) for acc in accs]
+            ratio = jnp.broadcast_to(gam_eight[n, :, lanes], (8, 128))
+            waves = [table[n, :, lanes] * coef[n, :, lanes] for coef, table, _ in terms]
+            for order in range(count):
+                for which, (_, _, ascending) in enumerate(terms):
+                    block = order if ascending else count - 1 - order
+                    accs[which][block] = accs[which][block] + waves[which]
+                    if order < count - 1:
+                        waves[which] = waves[which] * ratio
+            return tuple(tuple(acc) for acc in accs)
+
+        accs = lax.fori_loop(0, 16, body, ((zero,) * count,) * len(terms), unroll=4)
+        return [jnp.concatenate(acc, axis=0) for acc in accs]
 
     def dot(a, b):
         return jnp.dot(a, b, preferred_element_type=f32)
 
-    def spectrum_body(j, _):
+    for copy in small[2:]:
+        copy.wait()
+
+    def lag_body(j, _):
         lanes = lanes_of(j, mid)
-        taps = synth(coef_t, up_tab, lanes, mid, True)
+        table = fsub_ref[...]
+        spec_p = dot(table, prod2[:, lanes])
+        spec_c = dot(table, carr2[:, lanes])
+        real = jnp.zeros((sub_rows, mid), f32)
+        imag = jnp.zeros((sub_rows, mid), f32)
+        for part in range(parts):
+            lo = part * sub_rows
+            pr, pi = spec_p[lo : lo + sub_rows], spec_p[rows + lo : rows + lo + sub_rows]
+            cr, ci = spec_c[lo : lo + sub_rows], spec_c[rows + lo : rows + lo + sub_rows]
+            real = real + (cr * pr + ci * pi)
+            imag = imag + (ci * pr - cr * pi)
+        both = dot(isub_ref[...], jnp.concatenate([real.astype(bf16), imag.astype(bf16)], axis=0))
+        lag = both[:sub_rows] + both[sub_rows:]
+        lag_s[:, lanes] = lag
+        lag_w[:, lanes] = lag * up_weight[:sub_rows, :mid]
+        return 0
+
+    lax.fori_loop(0, channels // mid, lag_body, 0)
+
+    def moments_body(j, _):
+        lanes = lanes_of(j, wide)
+
+        def slope_body(part, _):
+            base = pl.multiple_of(part * sub_rows, sub_rows)
+            sub_s1[part, :, lanes], sub_b1[part, :, lanes] = horner([prod_w], [carr_w], base, lanes, wide)
+            return 0
+
+        lax.fori_loop(0, parts, slope_body, 0)
+        lag_0, lag_1 = horner([], [lag_s, lag_w], 0, lanes, wide)
+        for part in range(wide // 128):
+            cut = slice(part * 128, part * 128 + 128)
+            pair = j * (wide // 128) + part
+            own = lanes_of(pair, 128)
+            ratio = gam_sub[:, own]
+            total_0, total_1 = lag_0[:, cut], lag_1[:, cut]
+            state, slope = sub_s[0, :, own], sub_s1[0, :, own]
+            for q in range(1, parts):
+                c_state = sub_b[q, :, own]
+                total_0 = total_0 + c_state * state
+                total_1 = total_1 + sub_b1[q, :, own] * state + c_state * slope
+                slope = ratio * (slope + float(sub_rows) * state) + sub_s1[q, :, own]
+                state = ratio * state + sub_s[q, :, own]
+            c_slope = sub_b1[parts - 1, :, own]
+            c_state = sub_b[parts - 1, :, own]
+            for q in range(parts - 2, -1, -1):
+                c_slope = ratio * (c_slope + float(sub_rows) * c_state) + sub_b1[q, :, own]
+                c_state = ratio * c_state + sub_b[q, :, own]
+            tiles = [pack(x) for x in (slope, c_slope, total_0, total_1)]
+            for half in range(2):
+                send_l[2 * pair + half, 0] = jnp.concatenate(
+                    [tiles[0][half], tiles[1][half]], axis=0
+                ).astype(bf16)
+                send_l[2 * pair + half, 1] = jnp.concatenate(
+                    [tiles[2][half], tiles[3][half]], axis=0
+                ).astype(bf16)
+        return 0
+
+    lax.fori_loop(0, channels // wide, moments_body, 0)
+
+    def send_l_body(step, _):
+        owner = seq_peer(step)
+        pltpu.make_async_remote_copy(
+            src_ref=send_l.at[owner],
+            dst_ref=recv_l.at[me],
+            send_sem=l_send,
+            recv_sem=l_recv,
+            device_id={"seq": owner},
+            device_id_type=MESH,
+        ).start()
+        return 0
+
+    lax.fori_loop(1, groups, send_l_body, 0)
+    recv_l[me] = send_l[me]
+
+    def wait_bytes(ref, sem, count):
+        block = ref.at[pl.ds(0, count)]
+        pltpu.make_async_copy(block, block, sem).wait()
+
+    wait_bytes(recv_a, a_recv, groups - 1)
+    own_lanes = lanes_of(me // 2, 128)
+    is_left = lax.rem(me, 2) == 0
+
+    def own_pack(block):
+        first, second = pack(block)
+        return jnp.where(is_left, first, second)
+
+    own_decay = own_pack(rates_ref[:, own_lanes]) * inv_len
+    own_res = own_pack(res_ref[:, own_lanes])
+    span = jnp.exp(-own_decay * float(rows))
+    zero = jnp.zeros((8, 128), f32)
+
+    def up_scan(i, carry):
+        state, slope, total, moment = carry
+        p_in = recv_a[i, 0:8, :]
+        c_in = recv_a[i, 8:16, :]
+        send_b[i, 0:8, :] = state
+        total = total + c_in * state
+        moment = moment + c_in * slope
+        slope = span * (slope + state)
+        state = span * state + p_in
+        return state, slope, total, moment
+
+    _, _, total, moment = lax.fori_loop(0, groups, up_scan, (zero, zero, zero, zero), unroll=4)
+
+    def down_scan(i, state):
+        at = groups - 1 - i
+        send_b[at, 8:16, :] = state
+        return span * state + recv_a[at, 8:16, :]
+
+    lax.fori_loop(0, groups, down_scan, zero, unroll=4)
+
+    def send_b_body(step, _):
+        owner = seq_peer(step)
+        pltpu.make_async_remote_copy(
+            src_ref=send_b.at[owner],
+            dst_ref=recv_b.at[me],
+            send_sem=b_send,
+            recv_sem=b_recv,
+            device_id={"seq": owner},
+            device_id_type=MESH,
+        ).start()
+        return 0
+
+    lax.fori_loop(1, groups, send_b_body, 0)
+    recv_b[me] = send_b[me]
+
+    def skip_body(i, acc):
+        return acc + recv_a[i, 16:17, :]
+
+    skip_sum = lax.fori_loop(0, groups, skip_body, jnp.zeros((1, 128), f32))
+
+    def conv_body(j, _):
+        lanes = lanes_of(j, mid)
+        taps = jnp.concatenate(
+            [
+                synth([(coef_t, up_tab, True)], lanes_of(j * (mid // 128) + part, 128))[0]
+                for part in range(mid // 128)
+            ],
+            axis=1,
+        )
         high = taps.astype(bf16)
         low = (taps - high.astype(f32)).astype(bf16)
         table = fwd_ref[...]
@@ -278,102 +481,9 @@
 
         conv_s[:, lanes] = back_to_rows(pr * fr - pi * fi, pr * fi + pi * fr)
         back_s[:, lanes] = back_to_rows(cr * fr + ci * fi, ci * fr - cr * fi)
-        lag = back_to_rows(cr * pr + ci * pi, ci * pr - cr * pi)
-        lag_s[:, lanes] = lag
-        lag_w[:, lanes] = lag * up_weight[:, :mid]
-        return 0
-
-    lax.fori_loop(0, channels // mid, spectrum_body, 0)
-
-    def wait_bytes(ref, sem, count):
-        block = ref.at[pl.ds(0, count)]
-        pltpu.make_async_copy(block, block, sem).wait()
-
-    wait_bytes(recv_a, a_recv, groups - 1)
-    own_lanes = lanes_of(me // 2, 128)
-    is_left = lax.rem(me, 2) == 0
-
-    def own_pack(block):
-        first, second = pack(block)
-        return jnp.where(is_left, first, second)
-
-    own_decay = own_pack(rates_ref[:, own_lanes]) * inv_len
-    own_res = own_pack(res_ref[:, own_lanes])
-    span = jnp.exp(-own_decay * float(rows))
-    zero = jnp.zeros((8, 128), f32)
-
-    def up_scan(i, carry):
-        state, slope, total, moment = carry
-        p_in = recv_a[i, 0:8, :]
-        c_in = recv_a[i, 8:16, :]
-        send_b[i, 0:8, :] = state
-        total = total + c_in * state
-        moment = moment + c_in * slope
-        slope = span * (slope + state)
-        state = span * state + p_in
-        return state, slope, total, moment
-
-    _, _, total, moment = lax.fori_loop(0, groups, up_scan, (zero, zero, zero, zero), unroll=4)
-
-    def down_scan(i, state):
-        at = groups - 1 - i
-        send_b[at, 8:16, :] = state
-        return span * state + recv_a[at, 8:16, :]
-
-    lax.fori_loop(0, groups, down_scan, zero, unroll=4)
-
-    def send_b_body(step, _):
-        owner = seq_peer(step)
-        pltpu.make_async_remote_copy(
-            src_ref=send_b.at[owner],
-            dst_ref=recv_b.at[me],
-            send_sem=b_send,
-            recv_sem=b_recv,
-            device_id={"seq": owner},
-            device_id_type=MESH,
-        ).start()
-        return 0
-
-    lax.fori_loop(1, groups, send_b_body, 0)
-    recv_b[me] = send_b[me]
-
-    def skip_body(i, acc):
-        return acc + recv_a[i, 16:17, :]
-
-    skip_sum = lax.fori_loop(0, groups, skip_body, jnp.zeros((1, 128), f32))
-
-    def moments_body(j, _):
-        lanes = lanes_of(j, mid)
-        slope_p, slope_c, lag_0, lag_1 = horner([prod_w], [carr_w, lag_s, lag_w], lanes, mid)
-        for part in range(mid // 128):
-            cut = slice(part * 128, part * 128 + 128)
-            pair = j * (mid // 128) + part
-            tiles = [pack(x[:, cut]) for x in (slope_p, slope_c, lag_0, lag_1)]
-            for half in range(2):
-                send_l[2 * pair + half, 0] = jnp.concatenate(
-                    [tiles[0][half], tiles[1][half]], axis=0
-                ).astype(bf16)
-                send_l[2 * pair + half, 1] = jnp.concatenate(
-                    [tiles[2][half], tiles[3][half]], axis=0
-                ).astype(bf16)
-        return 0
-
-    lax.fori_loop(0, channels // mid, moments_body, 0)
-
-    def send_l_body(step, _):
-        owner = seq_peer(step)
-        pltpu.make_async_remote_copy(
-            src_ref=send_l.at[owner],
-            dst_ref=recv_l.at[me],
-            send_sem=l_send,
-            recv_sem=l_recv,
-            device_id={"seq": owner},
-            device_id_type=MESH,
-        ).start()
-        return 0
-
-    lax.fori_loop(1, groups, send_l_body, 0)
-    recv_l[me] = send_l[me]
+        return 0
+
+    lax.fori_loop(0, channels // mid, conv_body, 0)
 
     wait_bytes(recv_b, b_recv, groups - 1)
 
@@ -402,11 +512,12 @@
     def final_body(j, _):
         for part in range(mid // 128):
             lanes = lanes_of(j * (mid // 128) + part, 128)
-            conv = conv_s[:, lanes] + synth(coef_h, up_tab, lanes, 128, True)
-            back = back_s[:, lanes] + synth(coef_k, down_tab, lanes, 128, False)
+            far = synth([(coef_h, up_tab, True), (coef_k, down_tab, False)], lanes)
+            conv = conv_s[:, lanes] + far[0]
+            back = back_s[:, lanes] + far[1]
             gain = gain_ref[:, lanes]
-            y_out[:, lanes] = conv.astype(bf16).astype(f32) + gain * prod_f[:, lanes]
-            dz_out[:, lanes] = back.astype(bf16).astype(f32) + gain * carr_f[:, lanes]
+            y_out[:, lanes] = (conv.astype(bf16).astype(f32) + gain * prod_f[:, lanes]).astype(bf16)
+            dz_out[:, lanes] = (back.astype(bf16).astype(f32) + gain * carr_f[:, lanes]).astype(bf16)
         for copy in out_copies(j):
             copy.start()
         return 0
@@ -468,8 +579,8 @@
 
 
 def gate_kernel(cot, key, value, y, dz, grads, grad_q, grad_k, grad_v, grad_r, grad_l, grad_s):
-    dz_now = dz[...]
-    grad_q[...] = (cot[...].astype(f32) * y[...]).astype(bf16)
+    dz_now = dz[...].astype(f32)
+    grad_q[...] = (cot[...].astype(f32) * y[...].astype(f32)).astype(bf16)
     grad_k[...] = (dz_now * value[...].astype(f32)).astype(bf16)
     grad_v[...] = (dz_now * key[...].astype(f32)).astype(bf16)
 
@@ -486,10 +597,10 @@
     groups = lax.axis_size("seq")
     batch = lax.axis_size("dp")
     rows, channels = queries.shape[1:]
-    fwd, inv = dft_tables(rows)
+    sub_rows = 32
+    tables = [jnp.asarray(table) for table in stacked_tables(rows, sub_rows)]
     q, k, v, o = (x[0] for x in (queries, key_branch, value_branch, cotangent))
-    hbm = pl.BlockSpec(memory_space=pl.ANY)
-    vmem = pl.BlockSpec(memory_space=pltpu.VMEM)
+    hbm = pl.BlockSpec(memory_space=pltpu.HBM)
     big = pltpu.VMEM((rows, channels), f32)
     half = pltpu.VMEM((rows, channels), bf16)
     dma = pltpu.SemaphoreType.DMA
@@ -497,31 +608,36 @@
     y, dz, grads = pl.pallas_call(
         functools.partial(main_kernel, rows, channels, groups, batch),
         out_shape=[
-            jax.ShapeDtypeStruct((rows, channels), f32),
-            jax.ShapeDtypeStruct((rows, channels), f32),
+            jax.ShapeDtypeStruct((rows, channels), bf16),
+            jax.ShapeDtypeStruct((rows, channels), bf16),
             jax.ShapeDtypeStruct((24, 128), f32),
         ],
-        in_specs=[hbm] * 4 + [vmem] * 5,
-        out_specs=[hbm, hbm, vmem],
-        scratch_shapes=[half] * 4
+        in_specs=[hbm] * 11,
+        out_specs=[hbm, hbm, pl.BlockSpec(memory_space=pltpu.VMEM)],
+        scratch_shapes=[pltpu.VMEM((16, channels), f32)] * 2
+        + [pltpu.VMEM((1, channels), f32)]
+        + [pltpu.VMEM(table.shape, bf16) for table in tables]
+        + [half] * 4
         + [pltpu.VMEM((2 * rows, channels), bf16)] * 2
-        + [big] * 8
+        + [big] * 6
+        + [pltpu.VMEM((sub_rows, channels), f32)] * 2
         + [pltpu.VMEM((16, 8, channels), f32)] * 2
-        + [pltpu.VMEM((16, channels), f32)]
+        + [pltpu.VMEM((16, channels), f32)] * 2
+        + [pltpu.VMEM((rows // sub_rows, 16, channels), f32)] * 4
         + [pltpu.VMEM((16, 1, channels), f32)] * 4
-        + [big] * 2
+        + [half] * 2
         + [pltpu.VMEM((groups, 17, 128), f32)] * 2
         + [pltpu.VMEM((groups, 16, 128), f32)] * 2
         + [pltpu.VMEM((groups, 2, 16, 128), bf16)] * 2
         + [pltpu.VMEM((17, 128), f32), pltpu.VMEM((batch, 17, 128), f32)]
-        + [dma((4, chunks)), dma((2,))]
+        + [dma((4, chunks)), dma((7,)), dma((2,))]
         + [dma] * 8,
         compiler_params=pltpu.CompilerParams(
-            collective_id=0, has_side_effects=True, vmem_limit_bytes=48 * 2**20
+            collective_id=0, has_side_effects=True, vmem_limit_bytes=62 * 2**20
         ),
         name="hyena_main",
-    )(q, k, v, o, residues, rates, skip_gain[None, :], jnp.asarray(fwd), jnp.asarray(inv))
-    tile = min(32, rows)
+    )(q, k, v, o, residues, rates, skip_gain[None, :], *tables)
+    tile = min(64, rows)
     rowed = pl.BlockSpec((tile, channels), lambda i: (i, 0))
 
     def whole(*shape):
@@ -536,6 +652,7 @@
         + [jax.ShapeDtypeStruct((1, 64), f32)],
         in_specs=[rowed] * 5 + [whole(24, 128)],
         out_specs=[rowed] * 3 + [whole(16, 64), whole(16, 64), whole(1, 64)],
+        compiler_params=pltpu.CompilerParams(vmem_limit_bytes=62 * 2**20),
         name="hyena_gate",
     )(o, k, v, y, dz, grads)
     return gq[None], gk[None], gv[None], gr, gl, gs[0]

time: 64.4 us -> 52 us (0.81)
  local copies, waits for them, and re-layouts: 11 us -> 0 us
  Pallas kernels: 52.2 us -> 51.2 us
    unnamed x24 -> x0, local copies, waits for them, and re-layouts: 11 us -> none
    pallas_call x1, Pallas kernels: 4.1 us -> 2.77 us  [shards(): pl.pallas_call(gate_kernel, grid=(rows // tile,), out_shape=[wide16] * 3...]
where the time goes in v2:
time: 52 us; the launch traced here: 51.9 us
  Pallas kernels  51.2 us (98%)
  between operations  0.64 us (1%)
    pallas_call x1, Pallas kernels, shards(): pl.pallas_call(functools.partial(main_kernel, rows, channels, groups, bat...  48.4 us
    pallas_call x1, Pallas kernels, shards(): pl.pallas_call(gate_kernel, grid=(rows // tile,), out_shape=[wide16] * 3...  2.77 us

profile of v2, /device:TPU:1, one launch (start us, length us, event | category | flops | bytes accessed | tf_op | source)
XLA Modules:
  0.0 51.9 jit_solution(11415190340783877205)
XLA Ops:
  0.6 48.4 %hyena_main.1 = (bf16[128,2048]{1,0:T(8,128)(2,1)}, bf16[128,2048]{1,0:T(8,128)(2,1)}, f32[24,128]{1,0:T(8,128)}) custom-call(bf16[128,2048]{1,0:T(8,128)(2,1)} %bitcast.15, bf16[128,2048]{1,0:T(8,128)(2,1)} %bitcast.11, bf16[128,2048]{1,0:T(8,128)(2,1)} %bitcast.13, bf16[128,2048]{1,0:T(8,128)(2,1)} %bitcast.9, f32[16,2048]{1,0:T(8,128)} %res_hbm.1, ...), custom_call_target="tpu_custom_call" | custom-call | tf_op jit(solution)/shard_map/hyena_main/pallas_call | solution.py:608
  49.1 2.8 %hyena_gate.1 = (bf16[128,2048]{1,0:T(8,128)(2,1)}, bf16[128,2048]{1,0:T(8,128)(2,1)}, bf16[128,2048]{1,0:T(8,128)(2,1)}, f32[16,64]{1,0:T(8,128)}, f32[16,64]{1,0:T(8,128)}, /*index=5*/f32[1,64]{1,0:T(1,128)}) custom-call(bf16[128,2048]{1,0:T(8,128)(2,1)} %bitcast.10, bf16[128,2048]{1,0:T(8,128)(2,1)} %bitcast.12, bf16[128,2048]{1,0:T(8,128)(2,1)} %bitcast.14, ...), custom_call_target="tpu_custom_call" | custom-call | tf_op jit(solution)/shard_map/hyena_gate/pallas_call | solution.py:647

commit v3 on v2

v3 whole, which is shorter than its diff:
```python
import functools

import jax
import jax.numpy as jnp
import ml_dtypes
import numpy as np
from jax import lax
from jax.experimental import pallas as pl
from jax.experimental.pallas import tpu as pltpu
from jax.sharding import PartitionSpec as P

MESH = pl.DeviceIdType.MESH
f32 = jnp.float32
bf16 = jnp.bfloat16


def split_table(table):
    high = table.astype(ml_dtypes.bfloat16)
    low = (table - high.astype(np.float64)).astype(ml_dtypes.bfloat16)
    return high, low


def dft_tables(rows):
    odd = 2 * np.arange(rows)[:, None] + 1
    angle = np.pi / (2 * rows) * (odd * np.arange(rows)[None, :] % (4 * rows))
    forward = np.concatenate([np.cos(angle), -np.sin(angle)], axis=0)
    inverse = np.concatenate([np.cos(angle).T, -np.sin(angle).T], axis=1) / rows
    return forward, inverse


def stacked_tables(rows, sub_rows):
    forward, inverse = dft_tables(rows)
    sub_fwd, sub_inv = dft_tables(sub_rows)
    parts = rows // sub_rows
    blocks = np.zeros((2, sub_rows, parts, parts, sub_rows))
    for part in range(parts):
        blocks[:, :, part, part, :] = sub_fwd.reshape(2, sub_rows, sub_rows)
    blocks = blocks.transpose(0, 2, 1, 3, 4).reshape(2 * rows, rows)
    fwd = np.concatenate(split_table(forward), axis=1)
    inv = np.concatenate(split_table(inverse), axis=0)
    fwd_sub = np.concatenate(split_table(blocks), axis=1)
    inv_sub = np.concatenate(split_table(sub_inv), axis=0)
    return fwd, inv, fwd_sub, inv_sub


def main_kernel(
    rows,
    channels,
    groups,
    batch,
    q_hbm,
    k_hbm,
    v_hbm,
    o_hbm,
    res_hbm,
    rates_hbm,
    gain_hbm,
    fwd_hbm,
    inv_hbm,
    fsub_hbm,
    isub_hbm,
    y_hbm,
    dz_hbm,
    grad_ref,
    res_ref,
    rates_ref,
    gain_ref,
    fwd_ref,
    inv_ref,
    fsub_ref,
    isub_ref,
    q_in,
    k_in,
    v_in,
    o_in,
    prod_h,
    carr_h,
    prod_f,
    carr_f,
    conv_s,
    back_s,
    lag_s,
    up_tab,
    down_tab,
    gam_one,
    gam_sub,
    sub_s,
    sub_b,
    sub_s1,
    sub_b1,
    gam_eight,
    y_out,
    dz_out,
    span_t,
    send_a,
    pair_a,
    chip_a,
    recv_a,
    send_b,
    recv_b,
    send_l,
    pair_l,
    chip_l,
    recv_l,
    send_g,
    recv_g,
    in_sem,
    small_sem,
    out_sem,
    pa_send,
    pa_recv,
    a_send,
    a_recv,
    b_send,
    b_recv,
    f_send,
    f_recv,
    pl_send,
    pl_recv,
    l_send,
    l_recv,
    g_send,
    g_recv,
):
    length = rows * groups
    inv_len = 1.0 / length
    sub_rows = isub_ref.shape[0] // 2
    parts = rows // sub_rows
    ny = min(4, groups // 2)
    nx = groups // (2 * ny)
    chunks = nx
    wide = channels // chunks
    mid = min(256, channels)
    me = lax.axis_index("seq")
    me_b = lax.axis_index("dp")

    chips = groups // 2
    my_chip = me // 2
    core = lax.rem(me, 2)
    first_core = core == 0
    sibling = me + 1 - 2 * core

    def dp_peer(step):
        return lax.rem(me_b + step, batch)

    def lanes_of(index, size):
        return pl.ds(pl.multiple_of(index * size, size), size)

    my_x = me // (2 * ny)
    my_y = lax.rem(me // 2, ny)

    def spread(index, size):
        return lax.rem(index * (index + 1) // 2, size)

    def chip_at(index):
        x = lax.rem(my_x + spread(lax.rem(index, nx), nx), nx)
        y = lax.rem(my_y + spread(index // nx, ny), ny)
        return x * ny + y

    def chunk_at(step):
        return lax.rem(my_x + (chunks - 1 - step) * (chunks - step) // 2, chunks)

    def in_copies(step):
        lanes = lanes_of(chunk_at(step), wide)
        return [
            pltpu.make_async_copy(src.at[:, lanes], dst.at[:, lanes], in_sem.at[which, step])
            for which, (src, dst) in enumerate(
                ((k_hbm, k_in), (v_hbm, v_in), (o_hbm, o_in), (q_hbm, q_in))
            )
        ]

    small = [
        pltpu.make_async_copy(src, dst, small_sem.at[which])
        for which, (src, dst) in enumerate(
            (
                (rates_hbm, rates_ref),
                (res_hbm, res_ref),
                (gain_hbm, gain_ref),
                (fwd_hbm, fwd_ref),
                (inv_hbm, inv_ref),
                (fsub_hbm, fsub_ref),
                (isub_hbm, isub_ref),
            )
        )
    ]
    for copy in small[:2]:
        copy.start()
    for step in range(chunks):
        for copy in in_copies(step):
            copy.start()
    for copy in small[2:]:
        copy.start()

    barrier = pltpu.get_barrier_semaphore()

    def greet_chip(step, _):
        peer = 2 * lax.rem(my_chip + step, chips) + core
        pl.semaphore_signal(barrier, inc=1, device_id={"seq": peer}, device_id_type=MESH)
        return 0

    def greet_dp(step, _):
        pl.semaphore_signal(barrier, inc=1, device_id={"dp": dp_peer(step)}, device_id_type=MESH)
        return 0

    lax.fori_loop(1, chips, greet_chip, 0)
    pl.semaphore_signal(barrier, inc=1, device_id={"seq": sibling}, device_id_type=MESH)
    lax.fori_loop(1, batch, greet_dp, 0)

    for copy in small[:2]:
        copy.wait()
    decay_all = rates_ref[...] * inv_len
    gam_one[...] = jnp.exp(-decay_all)
    gam_sub[...] = jnp.exp(-float(sub_rows) * decay_all)
    lane = lax.broadcasted_iota(jnp.int32, (8, 128), 1)
    left = lane < 64

    def pack(block):
        top = block[0:8]
        low = block[8:16]
        return (
            jnp.where(left, top, pltpu.roll(low, 64, 1)),
            jnp.where(left, pltpu.roll(top, 64, 1), low),
        )

    def horner(up_refs, down_refs, base, lanes, width, weighted):
        gamma = gam_one[:, lanes]
        totals = [jnp.zeros((16, width), f32)] * (len(up_refs) + len(down_refs))
        ups = len(up_refs)
        row = lax.broadcasted_iota(jnp.int32, (8, width), 0).astype(f32)
        for i in range(sub_rows // 8):
            ups_in = [ref[pl.ds(pl.multiple_of(base + i * 8, 8), 8), lanes] for ref in up_refs]
            at = sub_rows - 8 - i * 8
            low = pl.multiple_of(base + at, 8)
            downs_in = [ref[pl.ds(low, 8), lanes] for ref in down_refs]
            if weighted:
                ups_in = [block * (float(sub_rows - i * 8) - row) for block in ups_in]
                downs_in = [
                    block * (float(at) + row) if flag else block
                    for block, flag in zip(downs_in, weighted)
                ]
            for r in range(8):
                for which, block in enumerate(ups_in):
                    totals[which] = totals[which] * gamma + block[r : r + 1]
                for which, block in enumerate(downs_in):
                    totals[ups + which] = totals[ups + which] * gamma + block[7 - r : 8 - r]
        return [t * gamma for t in totals[:ups]] + totals[ups:]

    for step in range(chunks):
        chunk = chunk_at(step)
        lanes = lanes_of(chunk, wide)
        for copy in in_copies(step):
            copy.wait()
        prod = (k_in[:, lanes].astype(f32) * v_in[:, lanes].astype(f32)).astype(bf16)
        carr = (o_in[:, lanes].astype(f32) * q_in[:, lanes].astype(f32)).astype(bf16)
        prod_h[:, lanes] = prod
        carr_h[:, lanes] = carr
        prod_32 = prod.astype(f32)
        carr_32 = carr.astype(f32)
        prod_f[:, lanes] = prod_32
        carr_f[:, lanes] = carr_32
        skip = jnp.sum(prod_32 * carr_32, axis=0, keepdims=True)

        def state_body(part, _):
            base = pl.multiple_of(part * sub_rows, sub_rows)
            sub_s[part, :, lanes], sub_b[part, :, lanes] = horner(
                [prod_f], [carr_f], base, lanes, wide, None
            )
            return 0

        lax.fori_loop(0, parts, state_body, 0)
        ratio = gam_sub[:, lanes]
        state_p = sub_s[0, :, lanes]
        state_c = sub_b[parts - 1, :, lanes]
        for part in range(1, parts):
            state_p = state_p * ratio + sub_s[part, :, lanes]
            state_c = state_c * ratio + sub_b[parts - 1 - part, :, lanes]
        for part in range(wide // 128):
            cut = slice(part * 128, part * 128 + 128)
            pair = chunk * (wide // 128) + part
            for half, (p_tile, c_tile) in enumerate(zip(pack(state_p[:, cut]), pack(state_c[:, cut]))):
                send_a[half, pair, 0:8, :] = p_tile
                send_a[half, pair, 8:16, :] = c_tile
            row = skip[:, cut]
            send_a[0, pair, 16:17, :] = row
            send_a[1, pair, 16:17, :] = pltpu.roll(row, 64, 1)

    pl.semaphore_wait(barrier, chips + batch - 1)

    def pair_copy(src, dst, send_sem, recv_sem):
        return pltpu.make_async_remote_copy(
            src_ref=src,
            dst_ref=dst,
            send_sem=send_sem,
            recv_sem=recv_sem,
            device_id={"seq": sibling},
            device_id_type=MESH,
        )

    pair_copy(send_a, pair_a, pa_send, pa_recv).start()

    def span_body(j, _):
        lanes = lanes_of(j, 128)
        span = jnp.exp(rates_ref[:, lanes] * (-inv_len * float(rows)))
        span_t[0, j], span_t[1, j] = pack(span)
        return 0

    lax.fori_loop(0, chips, span_body, 0, unroll=4)
    pltpu.make_async_copy(pair_a, pair_a, pa_recv).wait()

    def ordered(own, other):
        return jnp.where(first_core, own, other), jnp.where(first_core, other, own)

    def to_chip(src, dst, peer_chip, send_sem, recv_sem):
        return pltpu.make_async_remote_copy(
            src_ref=src.at[peer_chip],
            dst_ref=dst.at[my_chip],
            send_sem=send_sem,
            recv_sem=recv_sem,
            device_id={"seq": 2 * peer_chip + core},
            device_id_type=MESH,
        )

    def chip_states(i, _):
        j = chip_at(chips - 1 - i)
        span = span_t[core, j]
        p_first, p_second = ordered(send_a[core, j, 0:8, :], pair_a[core, j, 0:8, :])
        c_first, c_second = ordered(send_a[core, j, 8:16, :], pair_a[core, j, 8:16, :])
        chip_a[j, 0:8, :] = span * p_first + p_second
        chip_a[j, 8:16, :] = c_first + span * c_second
        chip_a[j, 16:17, :] = send_a[core, j, 16:17, :] + pair_a[core, j, 16:17, :]

        @pl.when(j != my_chip)
        def _():
            to_chip(chip_a, recv_a, j, a_send, a_recv).start()

        return 0

    lax.fori_loop(0, chips, chip_states, 0)
    recv_a[my_chip] = chip_a[my_chip]


    def synth(coefs, table, lanes, ascending):
        count = rows // 8
        waves = [table[n, :, lanes] * coefs[n // 8][n % 8 : n % 8 + 1] for n in range(16)]
        ratios = [jnp.broadcast_to(gam_eight[n, :, lanes], (8, 128)) for n in range(16)]
        blocks = []
        for order in range(count):
            terms = waves
            while len(terms) > 1:
                terms = [terms[i] + terms[i + 1] for i in range(0, len(terms), 2)]
            blocks.append(terms[0])
            if order < count - 1:
                waves = [wave * ratio for wave, ratio in zip(waves, ratios)]
        return jnp.concatenate(blocks if ascending else blocks[::-1], axis=0)

    def dot(a, b):
        return jnp.dot(a, b, preferred_element_type=f32)

    for copy in small[2:]:
        copy.wait()

    def lag_body(j, _):
        lanes = lanes_of(j, mid)
        table = fsub_ref[...]
        prod = prod_h[:, lanes]
        carr = carr_h[:, lanes]
        spec_p = dot(table, jnp.concatenate([prod, prod], axis=0))
        spec_c = dot(table, jnp.concatenate([carr, carr], axis=0))
        real = jnp.zeros((sub_rows, mid), f32)
        imag = jnp.zeros((sub_rows, mid), f32)
        for part in range(parts):
            lo = part * sub_rows
            pr, pi = spec_p[lo : lo + sub_rows], spec_p[rows + lo : rows + lo + sub_rows]
            cr, ci = spec_c[lo : lo + sub_rows], spec_c[rows + lo : rows + lo + sub_rows]
            real = real + (cr * pr + ci * pi)
            imag = imag + (ci * pr - cr * pi)
        both = dot(isub_ref[...], jnp.concatenate([real.astype(bf16), imag.astype(bf16)], axis=0))
        lag_s[:, lanes] = both[:sub_rows] + both[sub_rows:]
        return 0

    lax.fori_loop(0, channels // mid, lag_body, 0)

    def moments_body(j, _):
        lanes = lanes_of(j, wide)

        def slope_body(part, _):
            base = pl.multiple_of(part * sub_rows, sub_rows)
            sub_s1[part, :, lanes], sub_b1[part, :, lanes] = horner(
                [prod_f], [carr_f], base, lanes, wide, (True,)
            )
            return 0

        lax.fori_loop(0, parts, slope_body, 0)
        lag_0, lag_1 = horner([], [lag_s, lag_s], 0, lanes, wide, (False, True))
        for part in range(wide // 128):
            cut = slice(part * 128, part * 128 + 128)
            pair = j * (wide // 128) + part
            own = lanes_of(pair, 128)
            ratio = gam_sub[:, own]
            total_0, total_1 = lag_0[:, cut], lag_1[:, cut]
            state, slope = sub_s[0, :, own], sub_s1[0, :, own]
            for q in range(1, parts):
                c_state = sub_b[q, :, own]
                total_0 = total_0 + c_state * state
                total_1 = total_1 + sub_b1[q, :, own] * state + c_state * slope
                slope = ratio * (slope + float(sub_rows) * state) + sub_s1[q, :, own]
                state = ratio * state + sub_s[q, :, own]
            c_slope = sub_b1[parts - 1, :, own]
            c_state = sub_b[parts - 1, :, own]
            for q in range(parts - 2, -1, -1):
                c_slope = ratio * (c_slope + float(sub_rows) * c_state) + sub_b1[q, :, own]
                c_state = ratio * c_state + sub_b[q, :, own]
            tiles = [pack(x) for x in (slope, c_slope, total_0, total_1)]
            for half in range(2):
                send_l[half, pair, 0] = jnp.concatenate(
                    [tiles[0][half], tiles[1][half]], axis=0
                ).astype(bf16)
                send_l[half, pair, 1] = jnp.concatenate(
                    [tiles[2][half], tiles[3][half]], axis=0
                ).astype(bf16)
        return 0

    lax.fori_loop(0, channels // wide, moments_body, 0)

    pair_copy(send_l.at[1 - core], pair_l, pl_send, pl_recv).start()

    def table_body(n, _):
        rate = rates_ref[pl.ds(n, 1), :] * inv_len
        sub = lax.broadcasted_iota(jnp.int32, (8, channels), 0).astype(f32)
        gam_eight[n] = jnp.exp(-8.0 * rate)
        up_tab[n] = jnp.exp(-rate * sub)
        down_tab[n] = jnp.exp(-rate * (8.0 - sub))
        return 0

    lax.fori_loop(0, 16, table_body, 0)

    pltpu.make_async_copy(pair_l, pair_l, pl_recv).wait()

    def chip_sums(i, _):
        j = chip_at(chips - 1 - i)
        span = span_t[core, j]
        p_first, _ = ordered(send_a[core, j, 0:8, :], pair_a[core, j, 0:8, :])
        _, c_second = ordered(send_a[core, j, 8:16, :], pair_a[core, j, 8:16, :])
        own_slope, own_lag = send_l[core, j, 0].astype(f32), send_l[core, j, 1].astype(f32)
        pair_slope, pair_lag = pair_l[j, 0].astype(f32), pair_l[j, 1].astype(f32)
        sp_first, sp_second = ordered(own_slope[0:8], pair_slope[0:8])
        sc_first, sc_second = ordered(own_slope[8:16], pair_slope[8:16])
        lags = own_lag + pair_lag
        chip_l[j, 0] = jnp.concatenate(
            [
                span * (sp_first + float(rows) * p_first) + sp_second,
                sc_first + span * (sc_second + float(rows) * c_second),
            ],
            axis=0,
        ).astype(bf16)
        chip_l[j, 1] = jnp.concatenate(
            [
                lags[0:8] + c_second * p_first,
                lags[8:16] + (sc_second * p_first + c_second * sp_first),
            ],
            axis=0,
        ).astype(bf16)

        @pl.when(j != my_chip)
        def _():
            to_chip(chip_l, recv_l, j, l_send, l_recv).start()

        return 0

    lax.fori_loop(0, chips, chip_sums, 0)
    recv_l[my_chip] = chip_l[my_chip]

    def conv_body(j, _):
        lanes = lanes_of(j, mid)
        taps = jnp.concatenate(
            [
                synth((res_ref[0:8, own], res_ref[8:16, own]), up_tab, own, True)
                for own in [lanes_of(j * (mid // 128) + part, 128) for part in range(mid // 128)]
            ],
            axis=1,
        )
        high = taps.astype(bf16)
        low = (taps - high.astype(f32)).astype(bf16)
        table = fwd_ref[...]
        filt = dot(table, jnp.concatenate([high, high], axis=0)) + dot(table[:, :rows], low)
        prod = prod_h[:, lanes]
        carr = carr_h[:, lanes]
        spec_p = dot(table, jnp.concatenate([prod, prod], axis=0))
        spec_c = dot(table, jnp.concatenate([carr, carr], axis=0))
        fr, fi = filt[:rows], filt[rows:]
        pr, pi = spec_p[:rows], spec_p[rows:]
        cr, ci = spec_c[:rows], spec_c[rows:]
        inverse = inv_ref[...]

        def back_to_rows(real, imag):
            spec = jnp.concatenate([real.astype(bf16), imag.astype(bf16)], axis=0)
            both = dot(inverse, spec)
            return both[:rows] + both[rows:]

        conv_s[:, lanes] = back_to_rows(pr * fr - pi * fi, pr * fi + pi * fr)
        back_s[:, lanes] = back_to_rows(cr * fr + ci * fi, ci * fr - cr * fi)
        return 0

    conv_steps = channels // mid
    conv_early = conv_steps // 2
    lax.fori_loop(0, conv_early, conv_body, 0)

    def wait_bytes(ref, sem, count):
        block = ref.at[pl.ds(0, count)]
        pltpu.make_async_copy(block, block, sem).wait()

    wait_bytes(recv_a, a_recv, chips - 1)
    own_lanes = lanes_of(my_chip, 128)

    def own_pack(block):
        first, second = pack(block)
        return jnp.where(first_core, first, second)

    own_decay = own_pack(rates_ref[:, own_lanes]) * inv_len
    own_res = own_pack(res_ref[:, own_lanes])
    span = jnp.exp(-own_decay * float(2 * rows))
    zero = jnp.zeros((8, 128), f32)

    def up_scan(i, carry):
        state, slope, total, moment = carry
        p_in = recv_a[i, 0:8, :]
        c_in = recv_a[i, 8:16, :]
        send_b[i, 0:8, :] = state
        total = total + c_in * state
        moment = moment + c_in * slope
        slope = span * (slope + state)
        state = span * state + p_in
        return state, slope, total, moment

    _, _, total, moment = lax.fori_loop(0, chips, up_scan, (zero, zero, zero, zero), unroll=4)

    def down_scan(i, state):
        at = chips - 1 - i
        send_b[at, 8:16, :] = state
        return span * state + recv_a[at, 8:16, :]

    lax.fori_loop(0, chips, down_scan, zero, unroll=4)

    def send_b_body(i, _):
        j = chip_at(chips - 1 - i)

        @pl.when(j != my_chip)
        def _():
            pltpu.make_async_remote_copy(
                src_ref=send_b.at[j],
                dst_ref=recv_b.at[core, my_chip],
                send_sem=b_send,
                recv_sem=b_recv.at[my_chip],
                device_id={"seq": 2 * j + core},
                device_id_type=MESH,
            ).start()

        return 0

    lax.fori_loop(0, chips, send_b_body, 0)
    recv_b[core, my_chip] = send_b[my_chip]

    def skip_body(i, acc):
        return acc + recv_a[i, 16:17, :]

    skip_sum = lax.fori_loop(0, chips, skip_body, jnp.zeros((1, 128), f32))

    lax.fori_loop(conv_early, conv_steps, conv_body, 0)

    wait_bytes(recv_l, l_recv, chips - 1)

    def combine_body(i, carry):
        grad_0, grad_1 = carry
        slopes = recv_l[i, 0].astype(f32)
        lags = recv_l[i, 1].astype(f32)
        grad_0 = grad_0 + lags[0:8]
        grad_1 = grad_1 + lags[8:16]
        grad_1 = grad_1 + slopes[8:16] * send_b[i, 0:8, :] + slopes[0:8] * send_b[i, 8:16, :]
        return grad_0, grad_1

    grad_0, grad_1 = lax.fori_loop(
        0, chips, combine_body, (total, float(2 * rows) * moment), unroll=4
    )
    send_g[0:8, :] = grad_0 * inv_len
    send_g[8:16, :] = -own_res * own_decay * grad_1 * inv_len
    send_g[16:17, :] = skip_sum * inv_len

    def send_g_body(step, _):
        pltpu.make_async_remote_copy(
            src_ref=send_g,
            dst_ref=recv_g.at[me_b],
            send_sem=g_send,
            recv_sem=g_recv,
            device_id={"dp": dp_peer(step)},
            device_id_type=MESH,
        ).start()
        return 0

    lax.fori_loop(1, batch, send_g_body, 0)
    recv_g[me_b] = send_g[...]
    def out_copies(j):
        lanes = lanes_of(j, 128)
        return [
            pltpu.make_async_copy(src.at[:, lanes], dst.at[:, lanes], out_sem.at[which])
            for which, (src, dst) in enumerate(((y_out, y_hbm), (dz_out, dz_hbm)))
        ]

    def forward(i):
        j = chip_at(i)
        block = recv_b.at[core, j]

        @pl.when(j != my_chip)
        def _():
            pltpu.make_async_copy(block, block, b_recv.at[j]).wait()

        pair_copy(block, block, f_send, f_recv.at[j]).start()

    ahead = min(3, chips)
    for i in range(ahead):
        forward(i)

    def final_body(i, _):
        @pl.when(i + ahead < chips)
        def _():
            forward(i + ahead)

        j = chip_at(i)
        other = recv_b.at[1 - core, j]
        pltpu.make_async_copy(other, other, f_recv.at[j]).wait()
        lanes = lanes_of(j, 128)
        res = res_ref[:, lanes]
        far = []
        for half, far_core, table, ascending in ((0, 1, up_tab, True), (8, 0, down_tab, False)):
            states = []
            for part in range(2):
                state = recv_b[part, j, half : half + 8, :]
                farther = span_t[part, j] * state + pair_a[part, j, half : half + 8, :]
                states.append(jnp.where(core == far_core, farther, state))
            first, second = states
            low = res[0:8] * jnp.where(left, first, pltpu.roll(second, 64, 1))
            high = res[8:16] * jnp.where(left, pltpu.roll(first, 64, 1), second)
            far.append(synth((low, high), table, lanes, ascending))
        conv = conv_s[:, lanes] + far[0]
        back = back_s[:, lanes] + far[1]
        gain = gain_ref[:, lanes]
        y_out[:, lanes] = (conv.astype(bf16).astype(f32) + gain * prod_f[:, lanes]).astype(bf16)
        dz_out[:, lanes] = (back.astype(bf16).astype(f32) + gain * carr_f[:, lanes]).astype(bf16)
        for copy in out_copies(j):
            copy.start()
        return 0

    lax.fori_loop(0, chips, final_body, 0)

    wait_bytes(recv_g, g_recv, batch - 1)

    def total_body(i, acc):
        return acc + recv_g[i]

    grad_ref[0:17, :] = lax.fori_loop(0, batch, total_body, jnp.zeros((17, 128), f32))

    pltpu.make_async_copy(send_a, send_a, pa_send).wait()
    pltpu.make_async_copy(pair_l, pair_l, pl_send).wait()
    wait_bytes(chip_a, a_send, chips - 1)
    wait_bytes(send_b, b_send, chips - 1)
    wait_bytes(chip_l, l_send, chips - 1)
    wait_bytes(send_b, f_send, chips)
    wait_bytes(recv_g, g_send, batch - 1)

    def drain(j, _):
        for copy in out_copies(j):
            copy.wait()
        return 0

    lax.fori_loop(0, chips, drain, 0)


def gate_kernel(cot, key, value, y, dz, grads, grad_q, grad_k, grad_v, grad_r, grad_l, grad_s):
    dz_now = dz[...].astype(f32)
    grad_q[...] = (cot[...].astype(f32) * y[...].astype(f32)).astype(bf16)
    grad_k[...] = (dz_now * value[...].astype(f32)).astype(bf16)
    grad_v[...] = (dz_now * key[...].astype(f32)).astype(bf16)

    @pl.when(pl.program_id(0) == 0)
    def _():
        for start, out in ((0, grad_r), (8, grad_l)):
            tile = grads[start : start + 8, :]
            out[0:8, :] = tile[:, 0:64]
            out[8:16, :] = pltpu.roll(tile, 64, 1)[:, 0:64]
        grad_s[...] = grads[16:17, 0:64]


def shards(queries, key_branch, value_branch, cotangent, residues, rates, skip_gain):
    groups = lax.axis_size("seq")
    batch = lax.axis_size("dp")
    rows, channels = queries.shape[1:]
    sub_rows = 32
    tables = [jnp.asarray(table) for table in stacked_tables(rows, sub_rows)]
    q, k, v, o = (x[0] for x in (queries, key_branch, value_branch, cotangent))
    hbm = pl.BlockSpec(memory_space=pltpu.HBM)
    big = pltpu.VMEM((rows, channels), f32)
    half = pltpu.VMEM((rows, channels), bf16)
    dma = pltpu.SemaphoreType.DMA
    chips = groups // 2
    chunks = chips // min(4, chips)
    y, dz, grads = pl.pallas_call(
        functools.partial(main_kernel, rows, channels, groups, batch),
        out_shape=[
            jax.ShapeDtypeStruct((rows, channels), bf16),
            jax.ShapeDtypeStruct((rows, channels), bf16),
            jax.ShapeDtypeStruct((24, 128), f32),
        ],
        in_specs=[hbm] * 11,
        out_specs=[hbm, hbm, pl.BlockSpec(memory_space=pltpu.VMEM)],
        scratch_shapes=[pltpu.VMEM((16, channels), f32)] * 2
        + [pltpu.VMEM((1, channels), f32)]
        + [pltpu.VMEM(table.shape, bf16) for table in tables]
        + [half] * 6
        + [big] * 4
        + [pltpu.VMEM((sub_rows, channels), f32)]
        + [pltpu.VMEM((16, 8, channels), f32)] * 2
        + [pltpu.VMEM((16, channels), f32)] * 2
        + [pltpu.VMEM((rows // sub_rows, 16, channels), f32)] * 4
        + [pltpu.VMEM((16, 1, channels), f32)]
        + [half] * 2
        + [pltpu.VMEM((2, chips, 8, 128), f32)]
        + [pltpu.VMEM((2, chips, 17, 128), f32)] * 2
        + [pltpu.VMEM((chips, 17, 128), f32)] * 2
        + [pltpu.VMEM((chips, 16, 128), f32)]
        + [pltpu.VMEM((2, chips, 16, 128), f32)]
        + [pltpu.VMEM((2, chips, 2, 16, 128), bf16)]
        + [pltpu.VMEM((chips, 2, 16, 128), bf16)] * 3
        + [pltpu.VMEM((17, 128), f32), pltpu.VMEM((batch, 17, 128), f32)]
        + [dma((4, chunks)), dma((7,)), dma((2,))]
        + [dma] * 5
        + [dma((chips,)), dma, dma((chips,))]
        + [dma] * 6,
        compiler_params=pltpu.CompilerParams(
            collective_id=0, has_side_effects=True, vmem_limit_bytes=62 * 2**20
        ),
        name="hyena_main",
    )(q, k, v, o, residues, rates, skip_gain[None, :], *tables)
    tile = min(64, rows)
    rowed = pl.BlockSpec((tile, channels), lambda i: (i, 0))

    def whole(*shape):
        return pl.BlockSpec(shape, lambda i: (0, 0))

    wide16 = jax.ShapeDtypeStruct((rows, channels), bf16)
    gq, gk, gv, gr, gl, gs = pl.pallas_call(
        gate_kernel,
        grid=(rows // tile,),
        out_shape=[wide16] * 3
        + [jax.ShapeDtypeStruct((16, 64), f32)] * 2
        + [jax.ShapeDtypeStruct((1, 64), f32)],
        in_specs=[rowed] * 5 + [whole(24, 128)],
        out_specs=[rowed] * 3 + [whole(16, 64), whole(16, 64), whole(1, 64)],
        compiler_params=pltpu.CompilerParams(vmem_limit_bytes=62 * 2**20),
        name="hyena_gate",
    )(o, k, v, y, dz, grads)
    return gq[None], gk[None], gv[None], gr, gl, gs[0]


def solution(mesh):
    row_spec = P("dp", "seq", None)
    return jax.shard_map(
        shards,
        mesh=mesh,
        in_specs=(row_spec,) * 4 + (P(),) * 3,
        out_specs=(row_spec,) * 3 + (P(None, "seq"), P(None, "seq"), P("seq")),
        check_vma=False,
    )
```

time: 52 us -> 44.3 us (0.85)
  Pallas kernels: 51.2 us -> 43.5 us
    pallas_call x1, Pallas kernels: 48.4 us -> 40.7 us  [shards(): pl.pallas_call(functools.partial(main_kernel, rows, channels, groups, bat...]
where the time goes in v3:
time: 44.3 us; the launch traced here: 44.2 us
  Pallas kernels  43.5 us (98%)
  between operations  0.64 us (1%)
    pallas_call x1, Pallas kernels, shards(): pl.pallas_call(functools.partial(main_kernel, rows, channels, groups, bat...  40.7 us
    pallas_call x1, Pallas kernels, shards(): pl.pallas_call(gate_kernel, grid=(rows // tile,), out_shape=[wide16] * 3...  2.77 us

profile of v3, /device:TPU:1, one launch (start us, length us, event | category | flops | bytes accessed | tf_op | source)
XLA Modules:
  0.0 44.2 jit_solution(14708593608025119890)
XLA Ops:
  0.6 40.7 %hyena_main.1 = (bf16[128,2048]{1,0:T(8,128)(2,1)}, bf16[128,2048]{1,0:T(8,128)(2,1)}, f32[24,128]{1,0:T(8,128)}) custom-call(bf16[128,2048]{1,0:T(8,128)(2,1)} %bitcast.15, bf16[128,2048]{1,0:T(8,128)(2,1)} %bitcast.11, bf16[128,2048]{1,0:T(8,128)(2,1)} %bitcast.13, bf16[128,2048]{1,0:T(8,128)(2,1)} %bitcast.9, f32[16,2048]{1,0:T(8,128)} %res_hbm.1, ...), custom_call_target="tpu_custom_call" | custom-call | tf_op jit(solution)/shard_map/hyena_main/pallas_call | solution.py:705
  41.4 2.8 %hyena_gate.1 = (bf16[128,2048]{1,0:T(8,128)(2,1)}, bf16[128,2048]{1,0:T(8,128)(2,1)}, bf16[128,2048]{1,0:T(8,128)(2,1)}, f32[16,64]{1,0:T(8,128)}, f32[16,64]{1,0:T(8,128)}, /*index=5*/f32[1,64]{1,0:T(1,128)}) custom-call(bf16[128,2048]{1,0:T(8,128)(2,1)} %bitcast.10, bf16[128,2048]{1,0:T(8,128)(2,1)} %bitcast.12, bf16[128,2048]{1,0:T(8,128)(2,1)} %bitcast.14, ...), custom_call_target="tpu_custom_call" | custom-call | tf_op jit(solution)/shard_map/hyena_gate/pallas_call | solution.py:749

commit v4 on v3

--- a/solution.py
+++ b/solution.py
@@ -88,6 +88,8 @@
     sub_b,
     sub_s1,
     sub_b1,
+    lag_0,
+    lag_1,
     gam_eight,
     y_out,
     dz_out,
@@ -130,7 +132,7 @@
     nx = groups // (2 * ny)
     chunks = nx
     wide = channels // chunks
-    mid = min(256, channels)
+    mid = min(512, channels)
     me = lax.axis_index("seq")
     me_b = lax.axis_index("dp")
 
@@ -222,28 +224,24 @@
             jnp.where(left, pltpu.roll(top, 64, 1), low),
         )
 
-    def horner(up_refs, down_refs, base, lanes, width, weighted):
+    def horner(jobs, lanes, width):
         gamma = gam_one[:, lanes]
-        totals = [jnp.zeros((16, width), f32)] * (len(up_refs) + len(down_refs))
-        ups = len(up_refs)
+        totals = [jnp.zeros((16, width), f32)] * len(jobs)
         row = lax.broadcasted_iota(jnp.int32, (8, width), 0).astype(f32)
         for i in range(sub_rows // 8):
-            ups_in = [ref[pl.ds(pl.multiple_of(base + i * 8, 8), 8), lanes] for ref in up_refs]
             at = sub_rows - 8 - i * 8
-            low = pl.multiple_of(base + at, 8)
-            downs_in = [ref[pl.ds(low, 8), lanes] for ref in down_refs]
-            if weighted:
-                ups_in = [block * (float(sub_rows - i * 8) - row) for block in ups_in]
-                downs_in = [
-                    block * (float(at) + row) if flag else block
-                    for block, flag in zip(downs_in, weighted)
-                ]
+            blocks = []
+            for ref, base, up, weighted in jobs:
+                start = pl.multiple_of(base + (i * 8 if up else at), 8)
+                block = ref[pl.ds(start, 8), lanes]
+                if weighted:
+                    block = block * (float(sub_rows - i * 8) - row if up else float(at) + row)
+                blocks.append(block)
             for r in range(8):
-                for which, block in enumerate(ups_in):
-                    totals[which] = totals[which] * gamma + block[r : r + 1]
-                for which, block in enumerate(downs_in):
-                    totals[ups + which] = totals[ups + which] * gamma + block[7 - r : 8 - r]
-        return [t * gamma for t in totals[:ups]] + totals[ups:]
+                for which, (job, block) in enumerate(zip(jobs, blocks)):
+                    x = block[r : r + 1] if job[2] else block[7 - r : 8 - r]
+                    totals[which] = totals[which] * gamma + x
+        return [t * gamma if job[2] else t for t, job in zip(totals, jobs)]
 
     for step in range(chunks):
         chunk = chunk_at(step)
@@ -263,7 +261,7 @@
         def state_body(part, _):
             base = pl.multiple_of(part * sub_rows, sub_rows)
             sub_s[part, :, lanes], sub_b[part, :, lanes] = horner(
-                [prod_f], [carr_f], base, lanes, wide, None
+                [(prod_f, base, True, False), (carr_f, base, False, False)], lanes, wide
             )
             return 0
 
@@ -320,22 +318,34 @@
             device_id_type=MESH,
         )
 
-    def chip_states(i, _):
-        j = chip_at(chips - 1 - i)
+    group = min(4, chips)
+
+    def by_groups(compute, store, send):
+        def body(i, _):
+            at = [chip_at(chips - 1 - (group * i + part)) for part in range(group)]
+            results = [compute(j) for j in at]
+            for j, result in zip(at, results):
+                store(j, result)
+            for j in at:
+                pl.when(j != my_chip)(functools.partial(send, j))
+            return 0
+
+        lax.fori_loop(0, chips // group, body, 0)
+
+    def chip_states(j):
         span = span_t[core, j]
-        p_first, p_second = ordered(send_a[core, j, 0:8, :], pair_a[core, j, 0:8, :])
-        c_first, c_second = ordered(send_a[core, j, 8:16, :], pair_a[core, j, 8:16, :])
-        chip_a[j, 0:8, :] = span * p_first + p_second
-        chip_a[j, 8:16, :] = c_first + span * c_second
-        chip_a[j, 16:17, :] = send_a[core, j, 16:17, :] + pair_a[core, j, 16:17, :]
-
-        @pl.when(j != my_chip)
-        def _():
-            to_chip(chip_a, recv_a, j, a_send, a_recv).start()
-
-        return 0
-
-    lax.fori_loop(0, chips, chip_states, 0)
+        own, other = send_a[core, j], pair_a[core, j]
+        p_first, p_second = ordered(own[0:8], other[0:8])
+        c_first, c_second = ordered(own[8:16], other[8:16])
+        return span * p_first + p_second, c_first + span * c_second, own[16:17] + other[16:17]
+
+    def store_states(j, result):
+        chip_a[j, 0:8, :], chip_a[j, 8:16, :], chip_a[j, 16:17, :] = result
+
+    def send_states(j):
+        to_chip(chip_a, recv_a, j, a_send, a_recv).start()
+
+    by_groups(chip_states, store_states, send_states)
     recv_a[my_chip] = chip_a[my_chip]
 
 
@@ -358,6 +368,11 @@
 
     for copy in small[2:]:
         copy.wait()
+
+    def lag_sums(j):
+        lanes = lanes_of(j, mid)
+        jobs = [(lag_s, 0, False, False), (lag_s, 0, False, True)]
+        lag_0[:, lanes], lag_1[:, lanes] = horner(jobs, lanes, mid)
 
     def lag_body(j, _):
         lanes = lanes_of(j, mid)
@@ -376,51 +391,57 @@
             imag = imag + (ci * pr - cr * pi)
         both = dot(isub_ref[...], jnp.concatenate([real.astype(bf16), imag.astype(bf16)], axis=0))
         lag_s[:, lanes] = both[:sub_rows] + both[sub_rows:]
-        return 0
-
+        for part in range(0, parts, 2):
+            jobs = []
+            for now in (part, part + 1):
+                jobs.append((prod_f, now * sub_rows, True, True))
+                jobs.append((carr_f, now * sub_rows, False, True))
+            slopes = horner(jobs, lanes, mid)
+            for now in range(2):
+                sub_s1[part + now, :, lanes] = slopes[2 * now]
+                sub_b1[part + now, :, lanes] = slopes[2 * now + 1]
+        lag_sums(jnp.maximum(j - 1, 0))
+        return 0
+
+    lag_s[:, 0:mid] = jnp.zeros((sub_rows, mid), f32)
     lax.fori_loop(0, channels // mid, lag_body, 0)
-
-    def moments_body(j, _):
-        lanes = lanes_of(j, wide)
-
-        def slope_body(part, _):
-            base = pl.multiple_of(part * sub_rows, sub_rows)
-            sub_s1[part, :, lanes], sub_b1[part, :, lanes] = horner(
-                [prod_f], [carr_f], base, lanes, wide, (True,)
-            )
-            return 0
-
-        lax.fori_loop(0, parts, slope_body, 0)
-        lag_0, lag_1 = horner([], [lag_s, lag_s], 0, lanes, wide, (False, True))
-        for part in range(wide // 128):
-            cut = slice(part * 128, part * 128 + 128)
-            pair = j * (wide // 128) + part
-            own = lanes_of(pair, 128)
-            ratio = gam_sub[:, own]
-            total_0, total_1 = lag_0[:, cut], lag_1[:, cut]
-            state, slope = sub_s[0, :, own], sub_s1[0, :, own]
-            for q in range(1, parts):
-                c_state = sub_b[q, :, own]
-                total_0 = total_0 + c_state * state
-                total_1 = total_1 + sub_b1[q, :, own] * state + c_state * slope
-                slope = ratio * (slope + float(sub_rows) * state) + sub_s1[q, :, own]
-                state = ratio * state + sub_s[q, :, own]
-            c_slope = sub_b1[parts - 1, :, own]
-            c_state = sub_b[parts - 1, :, own]
-            for q in range(parts - 2, -1, -1):
-                c_slope = ratio * (c_slope + float(sub_rows) * c_state) + sub_b1[q, :, own]
-                c_state = ratio * c_state + sub_b[q, :, own]
-            tiles = [pack(x) for x in (slope, c_slope, total_0, total_1)]
+    lag_sums(channels // mid - 1)
+
+    def moments_of(pair):
+        own = lanes_of(pair, 128)
+        ratio = gam_sub[:, own]
+        total_0, total_1 = lag_0[:, own], lag_1[:, own]
+        p_state = [sub_s[q, :, own] for q in range(parts)]
+        p_slope = [sub_s1[q, :, own] for q in range(parts)]
+        c_states = [sub_b[q, :, own] for q in range(parts)]
+        c_slopes = [sub_b1[q, :, own] for q in range(parts)]
+        state, slope = p_state[0], p_slope[0]
+        for q in range(1, parts):
+            total_0 = total_0 + c_states[q] * state
+            total_1 = total_1 + (c_slopes[q] * state + c_states[q] * slope)
+            slope = ratio * (slope + float(sub_rows) * state) + p_slope[q]
+            state = ratio * state + p_state[q]
+        c_slope, c_state = c_slopes[-1], c_states[-1]
+        for q in range(parts - 2, -1, -1):
+            c_slope = ratio * (c_slope + float(sub_rows) * c_state) + c_slopes[q]
+            c_state = ratio * c_state + c_states[q]
+        tiles = [pack(x) for x in (slope, c_slope, total_0, total_1)]
+        return [
+            jnp.concatenate([tiles[2 * which][half], tiles[2 * which + 1][half]], axis=0).astype(bf16)
+            for half in range(2)
+            for which in range(2)
+        ]
+
+    def moments_body(i, _):
+        pairs = [group * i + part for part in range(group)]
+        results = [moments_of(pair) for pair in pairs]
+        for pair, result in zip(pairs, results):
             for half in range(2):
-                send_l[half, pair, 0] = jnp.concatenate(
-                    [tiles[0][half], tiles[1][half]], axis=0
-                ).astype(bf16)
-                send_l[half, pair, 1] = jnp.concatenate(
-                    [tiles[2][half], tiles[3][half]], axis=0
-                ).astype(bf16)
-        return 0
-
-    lax.fori_loop(0, channels // wide, moments_body, 0)
+                for which in range(2):
+                    send_l[half, pair, which] = result[2 * half + which]
+        return 0
+
+    lax.fori_loop(0, chips // group, moments_body, 0)
 
     pair_copy(send_l.at[1 - core], pair_l, pl_send, pl_recv).start()
 
@@ -436,8 +457,7 @@
 
     pltpu.make_async_copy(pair_l, pair_l, pl_recv).wait()
 
-    def chip_sums(i, _):
-        j = chip_at(chips - 1 - i)
+    def chip_sums(j):
         span = span_t[core, j]
         p_first, _ = ordered(send_a[core, j, 0:8, :], pair_a[core, j, 0:8, :])
         _, c_second = ordered(send_a[core, j, 8:16, :], pair_a[core, j, 8:16, :])
@@ -446,28 +466,23 @@
         sp_first, sp_second = ordered(own_slope[0:8], pair_slope[0:8])
         sc_first, sc_second = ordered(own_slope[8:16], pair_slope[8:16])
         lags = own_lag + pair_lag
-        chip_l[j, 0] = jnp.concatenate(
-            [
-                span * (sp_first + float(rows) * p_first) + sp_second,
-                sc_first + span * (sc_second + float(rows) * c_second),
-            ],
-            axis=0,
-        ).astype(bf16)
-        chip_l[j, 1] = jnp.concatenate(
-            [
-                lags[0:8] + c_second * p_first,
-                lags[8:16] + (sc_second * p_first + c_second * sp_first),
-            ],
-            axis=0,
-        ).astype(bf16)
-
-        @pl.when(j != my_chip)
-        def _():
-            to_chip(chip_l, recv_l, j, l_send, l_recv).start()
-
-        return 0
-
-    lax.fori_loop(0, chips, chip_sums, 0)
+        slopes = [
+            span * (sp_first + float(rows) * p_first) + sp_second,
+            sc_first + span * (sc_second + float(rows) * c_second),
+        ]
+        sums = [
+            lags[0:8] + c_second * p_first,
+            lags[8:16] + (sc_second * p_first + c_second * sp_first),
+        ]
+        return [jnp.concatenate(tiles, axis=0).astype(bf16) for tiles in (slopes, sums)]
+
+    def store_sums(j, result):
+        chip_l[j, 0], chip_l[j, 1] = result
+
+    def send_sums(j):
+        to_chip(chip_l, recv_l, j, l_send, l_recv).start()
+
+    by_groups(chip_sums, store_sums, send_sums)
     recv_l[my_chip] = chip_l[my_chip]
 
     def conv_body(j, _):
@@ -502,7 +517,7 @@
         return 0
 
     conv_steps = channels // mid
-    conv_early = conv_steps // 2
+    conv_early = conv_steps // 4
     lax.fori_loop(0, conv_early, conv_body, 0)
 
     def wait_bytes(ref, sem, count):
@@ -598,6 +613,7 @@
 
     lax.fori_loop(1, batch, send_g_body, 0)
     recv_g[me_b] = send_g[...]
+
     def out_copies(j):
         lanes = lanes_of(j, 128)
         return [
@@ -649,7 +665,7 @@
             copy.start()
         return 0
 
-    lax.fori_loop(0, chips, final_body, 0)
+    lax.fori_loop(0, chips, final_body, 0, unroll=2)
 
     wait_bytes(recv_g, g_recv, batch - 1)
 
@@ -720,6 +736,7 @@
         + [pltpu.VMEM((16, 8, channels), f32)] * 2
         + [pltpu.VMEM((16, channels), f32)] * 2
         + [pltpu.VMEM((rows // sub_rows, 16, channels), f32)] * 4
+        + [pltpu.VMEM((16, channels), f32)] * 2
         + [pltpu.VMEM((16, 1, channels), f32)]
         + [half] * 2
         + [pltpu.VMEM((2, chips, 8, 128), f32)]

time: 44.3 us -> 42.2 us (0.953)
  Pallas kernels: 43.5 us -> 41.4 us
    pallas_call x1, Pallas kernels: 40.7 us -> 38.6 us  [shards(): pl.pallas_call(functools.partial(main_kernel, rows, channels, groups, bat...]
where the time goes in v4:
time: 42.2 us; the launch traced here: 42 us
  Pallas kernels  41.4 us (98%)
  between operations  0.64 us (2%)
    pallas_call x1, Pallas kernels, shards(): pl.pallas_call(functools.partial(main_kernel, rows, channels, groups, bat...  38.6 us
    pallas_call x1, Pallas kernels, shards(): pl.pallas_call(gate_kernel, grid=(rows // tile,), out_shape=[wide16] * 3...  2.77 us

profile of v4, /device:TPU:1, one launch (start us, length us, event | category | flops | bytes accessed | tf_op | source)
XLA Modules:
  0.0 42.0 jit_solution(2611330109656056711)
XLA Ops:
  0.6 38.6 %hyena_main.1 = (bf16[128,2048]{1,0:T(8,128)(2,1)}, bf16[128,2048]{1,0:T(8,128)(2,1)}, f32[24,128]{1,0:T(8,128)}) custom-call(bf16[128,2048]{1,0:T(8,128)(2,1)} %bitcast.15, bf16[128,2048]{1,0:T(8,128)(2,1)} %bitcast.11, bf16[128,2048]{1,0:T(8,128)(2,1)} %bitcast.13, bf16[128,2048]{1,0:T(8,128)(2,1)} %bitcast.9, f32[16,2048]{1,0:T(8,128)} %res_hbm.1, ...), custom_call_target="tpu_custom_call" | custom-call | tf_op jit(solution)/shard_map/hyena_main/pallas_call | solution.py:721
  39.2 2.8 %hyena_gate.1 = (bf16[128,2048]{1,0:T(8,128)(2,1)}, bf16[128,2048]{1,0:T(8,128)(2,1)}, bf16[128,2048]{1,0:T(8,128)(2,1)}, f32[16,64]{1,0:T(8,128)}, f32[16,64]{1,0:T(8,128)}, /*index=5*/f32[1,64]{1,0:T(1,128)}) custom-call(bf16[128,2048]{1,0:T(8,128)(2,1)} %bitcast.10, bf16[128,2048]{1,0:T(8,128)(2,1)} %bitcast.12, bf16[128,2048]{1,0:T(8,128)(2,1)} %bitcast.14, ...), custom_call_target="tpu_custom_call" | custom-call | tf_op jit(solution)/shard_map/hyena_gate/pallas_call | solution.py:766

commit v5 on v4

--- a/solution.py
+++ b/solution.py
@@ -187,11 +187,10 @@
     ]
     for copy in small[:2]:
         copy.start()
-    for step in range(chunks):
+    ready = min(2, chunks)
+    for step in range(ready):
         for copy in in_copies(step):
             copy.start()
-    for copy in small[2:]:
-        copy.start()
 
     barrier = pltpu.get_barrier_semaphore()
 
@@ -248,6 +247,9 @@
         lanes = lanes_of(chunk, wide)
         for copy in in_copies(step):
             copy.wait()
+        later = in_copies(step + ready) if step + ready < chunks else []
+        for copy in later + (small[2:] if step == chunks - 1 else []):
+            copy.start()
         prod = (k_in[:, lanes].astype(f32) * v_in[:, lanes].astype(f32)).astype(bf16)
         carr = (o_in[:, lanes].astype(f32) * q_in[:, lanes].astype(f32)).astype(bf16)
         prod_h[:, lanes] = prod
@@ -594,7 +596,7 @@
         return grad_0, grad_1
 
     grad_0, grad_1 = lax.fori_loop(
-        0, chips, combine_body, (total, float(2 * rows) * moment), unroll=4
+        0, chips, combine_body, (total, float(2 * rows) * moment), unroll=8
     )
     send_g[0:8, :] = grad_0 * inv_len
     send_g[8:16, :] = -own_res * own_decay * grad_1 * inv_len
@@ -667,13 +669,6 @@
 
     lax.fori_loop(0, chips, final_body, 0, unroll=2)
 
-    wait_bytes(recv_g, g_recv, batch - 1)
-
-    def total_body(i, acc):
-        return acc + recv_g[i]
-
-    grad_ref[0:17, :] = lax.fori_loop(0, batch, total_body, jnp.zeros((17, 128), f32))
-
     pltpu.make_async_copy(send_a, send_a, pa_send).wait()
     pltpu.make_async_copy(pair_l, pair_l, pl_send).wait()
     wait_bytes(chip_a, a_send, chips - 1)
@@ -688,6 +683,15 @@
         return 0
 
     lax.fori_loop(0, chips, drain, 0)
+
+    wait_bytes(recv_g, g_recv, batch - 1)
+
+    def total_body(i, acc):
+        return acc + recv_g[i]
+
+    grad_ref[0:17, :] = lax.fori_loop(
+        0, batch, total_body, jnp.zeros((17, 128), f32), unroll=True
+    )
 
 
 def gate_kernel(cot, key, value, y, dz, grads, grad_q, grad_k, grad_v, grad_r, grad_l, grad_s):

time: 42.2 us -> 42.3 us (level)
  no operation moved by 1% of the time
where the time goes in v5:
time: 42.3 us; the launch traced here: 42.1 us
  Pallas kernels  41.4 us (98%)
  between operations  0.64 us (2%)
    pallas_call x1, Pallas kernels, shards(): pl.pallas_call(functools.partial(main_kernel, rows, channels, groups, bat...  38.7 us
    pallas_call x1, Pallas kernels, shards(): pl.pallas_call(gate_kernel, grid=(rows // tile,), out_shape=[wide16] * 3...  2.77 us

profile of v5, /device:TPU:1, one launch (start us, length us, event | category | flops | bytes accessed | tf_op | source)
XLA Modules:
  0.0 42.1 jit_solution(5071827297687552871)
XLA Ops:
  0.6 38.7 %hyena_main.1 = (bf16[128,2048]{1,0:T(8,128)(2,1)}, bf16[128,2048]{1,0:T(8,128)(2,1)}, f32[24,128]{1,0:T(8,128)}) custom-call(bf16[128,2048]{1,0:T(8,128)(2,1)} %bitcast.15, bf16[128,2048]{1,0:T(8,128)(2,1)} %bitcast.11, bf16[128,2048]{1,0:T(8,128)(2,1)} %bitcast.13, bf16[128,2048]{1,0:T(8,128)(2,1)} %bitcast.9, f32[16,2048]{1,0:T(8,128)} %res_hbm.1, ...), custom_call_target="tpu_custom_call" | custom-call | tf_op jit(solution)/shard_map/hyena_main/pallas_call | solution.py:725
  39.3 2.8 %hyena_gate.1 = (bf16[128,2048]{1,0:T(8,128)(2,1)}, bf16[128,2048]{1,0:T(8,128)(2,1)}, bf16[128,2048]{1,0:T(8,128)(2,1)}, f32[16,64]{1,0:T(8,128)}, f32[16,64]{1,0:T(8,128)}, /*index=5*/f32[1,64]{1,0:T(1,128)}) custom-call(bf16[128,2048]{1,0:T(8,128)(2,1)} %bitcast.10, bf16[128,2048]{1,0:T(8,128)(2,1)} %bitcast.12, bf16[128,2048]{1,0:T(8,128)(2,1)} %bitcast.14, ...), custom_call_target="tpu_custom_call" | custom-call | tf_op jit(solution)/shard_map/hyena_gate/pallas_call | solution.py:770
